TPU v7x, 32 devices: a whole 2x2x4 slice. The times are simulated.
32 devices in a mesh: batch: 4 (over z), seq: 8 (over y, x, core).
Axes of the slice: x: 2, y: 2, z: 4, core: 2. Of those that a mesh axis runs over, the one named last changes fastest.
Arguments:
- tokens: bfloat16 [4, 1024, 768], P('batch', 'seq'), may hold values from -6 to 6
- skip_features: bfloat16 [4, 8192, 128], P('batch', 'seq'), may hold values from -6 to 6
- out_grad: bfloat16 [4, 8192, 128], P('batch', 'seq'), may hold values from -6 to 6
- crop_lengths: int32 [4, 4], P('batch'), may hold values from 1 to 61, as said below
- attend_gain: bfloat16 [768], P('seq'), may hold values from 0.25 to 1.75
- attend_shift: bfloat16 [768], P('seq'), may hold values from -4 to 4
- joint_weight: bfloat16 [768, 2304], P('seq'), may hold values from -0.21875 to 0.21875
- query_bias: bfloat16 [768], P('seq'), may hold values from -4 to 4
- value_bias: bfloat16 [768], P('seq'), may hold values from -4 to 4
- output_weight: bfloat16 [768, 768], P('seq'), may hold values from -6 to 6
- output_bias: bfloat16 [768], P('seq'), may hold values from -4 to 4
- mixer_gain: bfloat16 [768], P('seq'), may hold values from 0.25 to 1.75
- mixer_shift: bfloat16 [768], P('seq'), may hold values from -4 to 4
- expand_weight: bfloat16 [768, 3072], P('seq'), may hold values from -0.21875 to 0.21875
- expand_bias: bfloat16 [3072], P('seq'), may hold values from -4 to 4
- reduce_weight: bfloat16 [3072, 768], P('seq'), may hold values from -0.109375 to 0.109375
- reduce_bias: bfloat16 [768], P('seq'), may hold values from -4 to 4
- upsample_weight: bfloat16 [768, 1024], P('seq'), may hold values from -0.21875 to 0.21875
- kernel_first: bfloat16 [6912, 128], P('seq'), may hold values from -0.078125 to 0.078125
- kernel_second: bfloat16 [3456, 128], P('seq'), may hold values from -0.109375 to 0.109375
- residual_weight: bfloat16 [256, 128], P('seq'), may hold values from -0.375 to 0.375
Outputs:
- decoded: bfloat16 [4, 8192, 128], P('batch', 'seq')
- tokens_grad: float32 [4, 1024, 768], P('batch', 'seq')
- skip_grad: float32 [4, 8192, 128], P('batch', 'seq')
- attend_gain_grad: float32 [768], P('seq')
- attend_shift_grad: float32 [768], P('seq')
- joint_weight_grad: float32 [768, 2304], P('seq')
- query_bias_grad: float32 [768], P('seq')
- value_bias_grad: float32 [768], P('seq')
- output_weight_grad: float32 [768, 768], P('seq')
- output_bias_grad: float32 [768], P('seq')
- mixer_gain_grad: float32 [768], P('seq')
- mixer_shift_grad: float32 [768], P('seq')
- expand_weight_grad: float32 [768, 3072], P('seq')
- expand_bias_grad: float32 [3072], P('seq')
- reduce_weight_grad: float32 [3072, 768], P('seq')
- reduce_bias_grad: float32 [768], P('seq')
- upsample_weight_grad: float32 [768, 1024], P('seq')
- kernel_first_grad: float32 [6912, 128], P('seq')
- kernel_second_grad: float32 [3456, 128], P('seq')
- residual_weight_grad: float32 [256, 128], P('seq')
Inputs may be any that keep to these rules, and one draw needn't show every extreme that they name: `crop_lengths`: each group's 4 crop lengths are numbers of slices summing to 64. In each group one crop starts within the first 8 slices and ends within the last 8; each of the others is no longer than the whole part of 7 / 3 slices.
All inputs are finite; a program needn't handle non-finite values.
Results may differ from a plain program's by a relative error of at most 0.028.
Values may be sent and summed in bfloat16 or wider, within the bound.
No kernel may reach another device: no remote copies, remote signals or barrier semaphores. Data moves between devices by JAX's collectives and lax.ppermute only.
A program may use at most 256 MiB of HBM per device.

v0:
```python
import math

import jax
import jax.numpy as jnp
from jax import lax
from jax.sharding import PartitionSpec as P

HEADS = 12
PH = 4
CROPS = 4


PRECISE = lax.Precision.HIGHEST
EPS_LAYER = 1e-06
EPS_CROP = 1e-05


def with_halo(cells, sides, width):
    for axis, dim in sides:
        count = lax.axis_size(axis)
        ends = count - 1
        head = lax.slice_in_dim(cells, 0, width, axis=dim)
        tail = lax.slice_in_dim(cells, cells.shape[dim] - width, cells.shape[dim], axis=dim)
        cells = jnp.concatenate(
            [
                lax.ppermute(tail, axis, [(i, (i + 1) % count) for i in range(ends)]),
                cells,
                lax.ppermute(head, axis, [((i + 1) % count, i) for i in range(ends)]),
            ],
            axis=dim,
        )
    return cells


def exact_dot(first_arg, second_arg):
    return jnp.dot(first_arg, second_arg, precision=PRECISE)


def bf_dot(first_arg, second_arg):
    return jnp.dot(first_arg, second_arg, preferred_element_type=jnp.float32)


def cross_dot(first_arg, second_arg):
    return lax.dot_general(
        first_arg, second_arg, (((0,), (0,)), ((), ())), preferred_element_type=jnp.float32
    )


def back_dot(first_arg, second_arg):
    return lax.dot_general(
        first_arg, second_arg, (((1,), (1,)), ((), ())), preferred_element_type=jnp.float32
    )


def spread_rows(member, per_crop):
    return lax.dot_general(member, per_crop, (((0,), (0,)), ((), ())), precision=PRECISE)


def crops_of(lengths, indices):
    crop_ends = jnp.cumsum(lengths)
    return jnp.sum((indices[:, None] >= crop_ends[None, :]).astype(jnp.int32), axis=1)


def layer_norm(values, gain_vec, shift_vec):
    average = jnp.mean(values, axis=-1, keepdims=True)
    centred = values - average
    inv_std = lax.rsqrt(jnp.mean(centred * centred, axis=-1, keepdims=True) + EPS_LAYER)
    unit_rows = centred * inv_std
    return (unit_rows * gain_vec + shift_vec, unit_rows, inv_std)


def layer_back(upstream, unit_rows, inv_std, gain_vec):
    scaled = upstream * gain_vec
    return inv_std * (
        scaled
        - jnp.mean(scaled, axis=-1, keepdims=True)
        - unit_rows * jnp.mean(scaled * unit_rows, axis=-1, keepdims=True)
    )


def gelu_exact(values):
    return jax.nn.gelu(values, approximate=False)


def gelu_back(values, upstream):
    return jax.vjp(gelu_exact, values)[1](upstream)[0]


def with_rims(grid_field):
    extended = with_halo(grid_field, (("seq", 0),), 1)
    return jnp.pad(extended, ((0, 0), (1, 1), (1, 1), (0, 0)))


def planes(padded, keep_mask, layer_idx):
    depth_rows = keep_mask.shape[0]
    grid_high = padded.shape[1] - 2
    grid_wide = padded.shape[2] - 2
    slab_rows = padded[layer_idx : layer_idx + depth_rows] * keep_mask[:, None, None, None]
    pieces = [
        slab_rows[:, row_off : row_off + grid_high, col_off : col_off + grid_wide, :]
        for row_off in range(3)
        for col_off in range(3)
    ]
    return jnp.concatenate(pieces, axis=-1).reshape(depth_rows * grid_high * grid_wide, -1)


def forward_taps(weight):
    block_len = weight.shape[0] // 3
    return [weight[layer_idx * block_len : (layer_idx + 1) * block_len] for layer_idx in range(3)]


def backward_taps(weight, in_chans):
    cube = weight.reshape(3, 3, 3, in_chans, weight.shape[1])[::-1, ::-1, ::-1]
    turned = jnp.swapaxes(cube, 3, 4)
    return [turned[layer_idx].reshape(9 * weight.shape[1], in_chans) for layer_idx in range(3)]


def stencil(padded, keep_masks, matrices):
    running = None
    for layer_idx in range(3):
        term = bf_dot(planes(padded, keep_masks[layer_idx], layer_idx), matrices[layer_idx])
        running = term if running is None else running + term
    return running


def weight_grad(padded, keep_masks, upstream):
    return jnp.concatenate(
        [
            cross_dot(planes(padded, keep_masks[layer_idx], layer_idx), upstream)
            for layer_idx in range(3)
        ],
        axis=0,
    )


def crop_total(values):
    return lax.psum(values, "seq")


def crop_norm(values, member, counts):
    local_sum = exact_dot(member, values)
    sums = crop_total((local_sum,))[0]
    average = sums / counts
    centred = values - spread_rows(member, average)
    spread = lax.psum(exact_dot(member, centred * centred), "seq") / counts
    inv_rows = spread_rows(member, lax.rsqrt(spread + EPS_CROP))
    return (centred * inv_rows, inv_rows)


def crop_backnorm(upstream, unit_rows, inv_rows, member, counts):
    first_sum, cross_sum = crop_total(
        (exact_dot(member, upstream), exact_dot(member, upstream * unit_rows))
    )
    return inv_rows * (
        upstream
        - spread_rows(member, first_sum / counts)
        - unit_rows * spread_rows(member, cross_sum / counts)
    )


def on_device(
    tokens,
    skip_features,
    out_grad,
    crop_lengths,
    attend_gain,
    attend_shift,
    joint_weight,
    query_bias,
    value_bias,
    output_weight,
    output_bias,
    mixer_gain,
    mixer_shift,
    expand_weight,
    expand_bias,
    reduce_weight,
    reduce_bias,
    upsample_weight,
    kernel_first,
    kernel_second,
    residual_weight,
):
    shards = (
        attend_gain,
        attend_shift,
        joint_weight,
        query_bias,
        value_bias,
        output_weight,
        output_bias,
        mixer_gain,
        mixer_shift,
        expand_weight,
        expand_bias,
        reduce_weight,
        reduce_bias,
        upsample_weight,
        kernel_first,
        kernel_second,
        residual_weight,
    )
    gathered_w = (
        lax.all_gather(shards[0], "seq", axis=0, tiled=True),
        lax.all_gather(shards[1], "seq", axis=0, tiled=True),
        lax.all_gather(shards[2], "seq", axis=0, tiled=True),
        lax.all_gather(shards[3], "seq", axis=0, tiled=True),
        lax.all_gather(shards[4], "seq", axis=0, tiled=True),
        lax.all_gather(shards[5], "seq", axis=0, tiled=True),
        lax.all_gather(shards[6], "seq", axis=0, tiled=True),
        lax.all_gather(shards[7], "seq", axis=0, tiled=True),
        lax.all_gather(shards[8], "seq", axis=0, tiled=True),
        lax.all_gather(shards[9], "seq", axis=0, tiled=True),
        lax.all_gather(shards[10], "seq", axis=0, tiled=True),
        lax.all_gather(shards[11], "seq", axis=0, tiled=True),
        lax.all_gather(shards[12], "seq", axis=0, tiled=True),
        lax.all_gather(shards[13], "seq", axis=0, tiled=True),
        lax.all_gather(shards[14], "seq", axis=0, tiled=True),
        lax.all_gather(shards[15], "seq", axis=0, tiled=True),
        lax.all_gather(shards[16], "seq", axis=0, tiled=True),
    )
    (
        gain_a,
        shift_a,
        joint_w,
        query_b,
        value_b,
        out_w,
        out_b,
        gain_m,
        shift_m,
        expand_w,
        expand_b,
        reduce_w,
        reduce_b,
        upsample_w,
        kernel_one,
        kernel_two,
        residual_w,
    ) = gathered_w
    gain_a = gain_a.astype(jnp.float32)
    gain_m = gain_m.astype(jnp.float32)
    model_width = joint_w.shape[0]
    head_dim = model_width // HEADS
    score_scale = 1.0 / math.sqrt(head_dim)
    channels = residual_w.shape[1]
    plane_size = PH * PH
    tok_rows = tokens.shape[1]
    slices = tok_rows // plane_size
    depth_rows = 2 * slices
    positions = depth_rows * 4 * plane_size
    seq_index = lax.axis_index("seq")
    seq_devices = lax.axis_size("seq")
    lengths = crop_lengths[0]
    own_crop = jnp.repeat(
        crops_of(lengths, seq_index * slices + jnp.arange(slices, dtype=jnp.int32)), plane_size
    )
    all_crop = jnp.repeat(
        crops_of(lengths, jnp.arange(slices * seq_devices, dtype=jnp.int32)), plane_size
    )
    same_crop = (own_crop[:, None] == all_crop[None, :])[None]

    def split_heads(row_block):
        return row_block.reshape(row_block.shape[0], HEADS, head_dim)

    inputs = tokens[0].astype(jnp.float32)
    normed_a, unit_a, inv_a = layer_norm(inputs, gain_a, shift_a.astype(jnp.float32))
    normed_low = normed_a.astype(jnp.bfloat16)
    joint_out = bf_dot(normed_low, joint_w)
    queries = (joint_out[:, :model_width] + query_b.astype(jnp.float32)).astype(jnp.bfloat16)
    key_rows = joint_out[:, model_width : 2 * model_width].astype(jnp.bfloat16)
    value_rows = (joint_out[:, 2 * model_width :] + value_b.astype(jnp.float32)).astype(
        jnp.bfloat16
    )
    kv_pairs = jnp.concatenate([key_rows, value_rows], axis=1)
    kv_all = lax.all_gather(kv_pairs, "seq", axis=0, tiled=True)
    scores = (
        jnp.einsum(
            "the,lhe->htl",
            split_heads(queries),
            split_heads(kv_all[:, :model_width]),
            preferred_element_type=jnp.float32,
        )
        * score_scale
    )
    masked = jnp.where(same_crop, scores, -1000000000.0)
    highest = jnp.max(masked, axis=-1, keepdims=True)
    exp_scores = jnp.exp(masked - highest)
    totals = jnp.sum(exp_scores, axis=-1, keepdims=True)
    log_total = highest + jnp.log(totals)
    probability = (exp_scores / totals).astype(jnp.bfloat16)
    attended = (
        jnp.einsum(
            "htl,lhe->the",
            probability,
            split_heads(kv_all[:, model_width:]),
            preferred_element_type=jnp.float32,
        )
        .reshape(tok_rows, model_width)
        .astype(jnp.bfloat16)
    )
    middle = inputs + bf_dot(attended, out_w) + out_b.astype(jnp.float32)
    normed_m, unit_m, inv_m = layer_norm(middle, gain_m, shift_m.astype(jnp.float32))
    inner_low = normed_m.astype(jnp.bfloat16)
    expanded = bf_dot(inner_low, expand_w) + expand_b.astype(jnp.float32)
    activated = gelu_exact(expanded).astype(jnp.bfloat16)
    mixed_out = bf_dot(activated, reduce_w) + reduce_b.astype(jnp.float32)
    encoded = (middle + mixed_out).astype(jnp.bfloat16)
    up_rows = bf_dot(encoded, upsample_w).reshape(slices, PH, PH, 2, 2, 2, channels)
    upsampled = (
        up_rows.transpose(0, 3, 1, 4, 2, 5, 6)
        .reshape(depth_rows, 2 * PH, 2 * PH, channels)
        .astype(jnp.bfloat16)
    )
    joined = jnp.concatenate(
        [upsampled, skip_features[0].reshape(depth_rows, 2 * PH, 2 * PH, channels)], axis=-1
    )
    up_index = seq_index * depth_rows - 1 + jnp.arange(depth_rows + 2, dtype=jnp.int32)
    up_crop = crops_of(lengths, up_index // 2)
    keep_masks = [
        (up_crop[layer_idx : layer_idx + depth_rows] == up_crop[1 : 1 + depth_rows]).astype(
            jnp.bfloat16
        )
        for layer_idx in range(3)
    ]
    pos_crop = jnp.repeat(up_crop[1 : 1 + depth_rows], 4 * plane_size)
    member = (jnp.arange(CROPS, dtype=jnp.int32)[:, None] == pos_crop[None, :]).astype(jnp.float32)
    counts = (lengths * 8 * plane_size).astype(jnp.float32)[:, None]
    joined_rim = with_rims(joined)
    first_conv = stencil(joined_rim, keep_masks, forward_taps(kernel_one))
    first_unit, first_inv = crop_norm(first_conv, member, counts)
    act_one = gelu_exact(first_unit).astype(jnp.bfloat16)
    act_rim = with_rims(act_one.reshape(depth_rows, 2 * PH, 2 * PH, channels))
    second_conv = stencil(act_rim, keep_masks, forward_taps(kernel_two))
    second_unit, second_inv = crop_norm(second_conv, member, counts)
    joined_rows = joined.reshape(positions, 2 * channels)
    summed = second_unit + bf_dot(joined_rows, residual_w)
    decoded = gelu_exact(summed).astype(jnp.bfloat16)
    grad_summed = gelu_back(summed, out_grad[0].astype(jnp.float32))
    grad_resid = grad_summed.astype(jnp.bfloat16)
    grad_second = crop_backnorm(grad_summed, second_unit, second_inv, member, counts).astype(
        jnp.bfloat16
    )
    residual_grad = cross_dot(joined_rows, grad_resid)
    second_rim = with_rims(grad_second.reshape(depth_rows, 2 * PH, 2 * PH, channels))
    kernel_two_grad = weight_grad(act_rim, keep_masks, grad_second)
    grad_act = stencil(second_rim, keep_masks, backward_taps(kernel_two, channels))
    grad_first = crop_backnorm(
        gelu_back(first_unit, grad_act), first_unit, first_inv, member, counts
    ).astype(jnp.bfloat16)
    kernel_one_grad = weight_grad(joined_rim, keep_masks, grad_first)
    first_rim = with_rims(grad_first.reshape(depth_rows, 2 * PH, 2 * PH, channels))
    grad_joined = stencil(
        first_rim, keep_masks, backward_taps(kernel_one, 2 * channels)
    ) + back_dot(grad_resid, residual_w)
    skip_grad = grad_joined[:, channels:]
    grad_up = (
        grad_joined[:, :channels].astype(jnp.bfloat16).reshape(slices, 2, PH, 2, PH, 2, channels)
    )
    grad_up_rows = grad_up.transpose(0, 2, 4, 1, 3, 5, 6).reshape(tok_rows, 8 * channels)
    upsample_grad = cross_dot(encoded, grad_up_rows)
    grad_encoded = back_dot(grad_up_rows, upsample_w)
    grad_mixed = grad_encoded.astype(jnp.bfloat16)
    reduce_grad = cross_dot(activated, grad_mixed)
    reduce_bias_grad = jnp.sum(grad_mixed.astype(jnp.float32), axis=0)
    grad_expanded = gelu_back(expanded, back_dot(grad_mixed, reduce_w)).astype(jnp.bfloat16)
    expand_grad = cross_dot(inner_low, grad_expanded)
    expand_bias_grad = jnp.sum(grad_expanded.astype(jnp.float32), axis=0)
    grad_inner = back_dot(grad_expanded, expand_w)
    mixer_gain_grad = jnp.sum(grad_inner * unit_m, axis=0)
    mixer_shift_grad = jnp.sum(grad_inner, axis=0)
    grad_middle = grad_encoded + layer_back(grad_inner, unit_m, inv_m, gain_m)
    grad_branch = grad_middle.astype(jnp.bfloat16)
    output_grad = cross_dot(attended, grad_branch)
    output_bias_grad = jnp.sum(grad_branch.astype(jnp.float32), axis=0)
    grad_attended = back_dot(grad_branch, out_w).astype(jnp.bfloat16)
    kv_back = lax.all_gather(kv_pairs, "seq", axis=0, tiled=True)
    key_heads = split_heads(kv_back[:, :model_width])
    value_heads = split_heads(kv_back[:, model_width:])
    query_heads = split_heads(queries)
    again_scores = (
        jnp.einsum("the,lhe->htl", query_heads, key_heads, preferred_element_type=jnp.float32)
        * score_scale
    )
    again_prob = jnp.exp(jnp.where(same_crop, again_scores, -1000000000.0) - log_total)
    grad_weights = jnp.einsum(
        "the,lhe->htl", split_heads(grad_attended), value_heads, preferred_element_type=jnp.float32
    )
    inner_sum = jnp.sum(again_prob * grad_weights, axis=-1, keepdims=True)
    grad_scores = (again_prob * (grad_weights - inner_sum)).astype(jnp.bfloat16)
    grad_queries = (
        (
            jnp.einsum("htl,lhe->the", grad_scores, key_heads, preferred_element_type=jnp.float32)
            * score_scale
        )
        .reshape(tok_rows, model_width)
        .astype(jnp.bfloat16)
    )
    attended_heads = split_heads(grad_attended)
    prob_low = again_prob.astype(jnp.bfloat16)
    key_part = (
        jnp.einsum("htl,the->lhe", grad_scores, query_heads, preferred_element_type=jnp.float32)
        * score_scale
    )
    value_part = jnp.einsum(
        "htl,the->lhe", prob_low, attended_heads, preferred_element_type=jnp.float32
    )
    grad_pairs = lax.psum_scatter(
        jnp.concatenate(
            [
                key_part.reshape(tok_rows * lax.axis_size("seq"), model_width),
                value_part.reshape(tok_rows * lax.axis_size("seq"), model_width),
            ],
            axis=1,
        ).astype(jnp.bfloat16),
        "seq",
        scatter_dimension=0,
        tiled=True,
    ).astype(jnp.float32)
    grad_keys = grad_pairs[:, :model_width].astype(jnp.bfloat16)
    grad_values = grad_pairs[:, model_width:].astype(jnp.bfloat16)
    query_bias_grad = jnp.sum(grad_queries.astype(jnp.float32), axis=0)
    value_bias_grad = jnp.sum(grad_values.astype(jnp.float32), axis=0)
    grad_joint = jnp.concatenate([grad_queries, grad_keys, grad_values], axis=1)
    joint_grad = cross_dot(normed_low, grad_joint)
    grad_normed = back_dot(grad_joint, joint_w)
    attend_gain_grad = jnp.sum(grad_normed * unit_a, axis=0)
    attend_shift_grad = jnp.sum(grad_normed, axis=0)
    tokens_grad = grad_middle + layer_back(grad_normed, unit_a, inv_a, gain_a)
    partial_grads = (
        attend_gain_grad,
        attend_shift_grad,
        joint_grad,
        query_bias_grad,
        value_bias_grad,
        output_grad,
        output_bias_grad,
        mixer_gain_grad,
        mixer_shift_grad,
        expand_grad,
        expand_bias_grad,
        reduce_grad,
        reduce_bias_grad,
        upsample_grad,
        kernel_one_grad,
        kernel_two_grad,
        residual_grad,
    )
    group_grads = (
        lax.psum_scatter(
            partial_grads[0].astype(jnp.bfloat16), "seq", scatter_dimension=0, tiled=True
        ).astype(jnp.float32),
        lax.psum_scatter(
            partial_grads[1].astype(jnp.bfloat16), "seq", scatter_dimension=0, tiled=True
        ).astype(jnp.float32),
        lax.psum_scatter(
            partial_grads[2].astype(jnp.bfloat16), "seq", scatter_dimension=0, tiled=True
        ).astype(jnp.float32),
        lax.psum_scatter(
            partial_grads[3].astype(jnp.bfloat16), "seq", scatter_dimension=0, tiled=True
        ).astype(jnp.float32),
        lax.psum_scatter(
            partial_grads[4].astype(jnp.bfloat16), "seq", scatter_dimension=0, tiled=True
        ).astype(jnp.float32),
        lax.psum_scatter(
            partial_grads[5].astype(jnp.bfloat16), "seq", scatter_dimension=0, tiled=True
        ).astype(jnp.float32),
        lax.psum_scatter(
            partial_grads[6].astype(jnp.bfloat16), "seq", scatter_dimension=0, tiled=True
        ).astype(jnp.float32),
        lax.psum_scatter(
            partial_grads[7].astype(jnp.bfloat16), "seq", scatter_dimension=0, tiled=True
        ).astype(jnp.float32),
        lax.psum_scatter(
            partial_grads[8].astype(jnp.bfloat16), "seq", scatter_dimension=0, tiled=True
        ).astype(jnp.float32),
        lax.psum_scatter(
            partial_grads[9].astype(jnp.bfloat16), "seq", scatter_dimension=0, tiled=True
        ).astype(jnp.float32),
        lax.psum_scatter(
            partial_grads[10].astype(jnp.bfloat16), "seq", scatter_dimension=0, tiled=True
        ).astype(jnp.float32),
        lax.psum_scatter(
            partial_grads[11].astype(jnp.bfloat16), "seq", scatter_dimension=0, tiled=True
        ).astype(jnp.float32),
        lax.psum_scatter(
            partial_grads[12].astype(jnp.bfloat16), "seq", scatter_dimension=0, tiled=True
        ).astype(jnp.float32),
        lax.psum_scatter(
            partial_grads[13].astype(jnp.bfloat16), "seq", scatter_dimension=0, tiled=True
        ).astype(jnp.float32),
        lax.psum_scatter(
            partial_grads[14].astype(jnp.bfloat16), "seq", scatter_dimension=0, tiled=True
        ).astype(jnp.float32),
        lax.psum_scatter(
            partial_grads[15].astype(jnp.bfloat16), "seq", scatter_dimension=0, tiled=True
        ).astype(jnp.float32),
        lax.psum_scatter(
            partial_grads[16].astype(jnp.bfloat16), "seq", scatter_dimension=0, tiled=True
        ).astype(jnp.float32),
    )
    total_grads = (
        lax.psum(group_grads[0].astype(jnp.bfloat16), "batch").astype(jnp.float32),
        lax.psum(group_grads[1].astype(jnp.bfloat16), "batch").astype(jnp.float32),
        lax.psum(group_grads[2].astype(jnp.bfloat16), "batch").astype(jnp.float32),
        lax.psum(group_grads[3].astype(jnp.bfloat16), "batch").astype(jnp.float32),
        lax.psum(group_grads[4].astype(jnp.bfloat16), "batch").astype(jnp.float32),
        lax.psum(group_grads[5].astype(jnp.bfloat16), "batch").astype(jnp.float32),
        lax.psum(group_grads[6].astype(jnp.bfloat16), "batch").astype(jnp.float32),
        lax.psum(group_grads[7].astype(jnp.bfloat16), "batch").astype(jnp.float32),
        lax.psum(group_grads[8].astype(jnp.bfloat16), "batch").astype(jnp.float32),
        lax.psum(group_grads[9].astype(jnp.bfloat16), "batch").astype(jnp.float32),
        lax.psum(group_grads[10].astype(jnp.bfloat16), "batch").astype(jnp.float32),
        lax.psum(group_grads[11].astype(jnp.bfloat16), "batch").astype(jnp.float32),
        lax.psum(group_grads[12].astype(jnp.bfloat16), "batch").astype(jnp.float32),
        lax.psum(group_grads[13].astype(jnp.bfloat16), "batch").astype(jnp.float32),
        lax.psum(group_grads[14].astype(jnp.bfloat16), "batch").astype(jnp.float32),
        lax.psum(group_grads[15].astype(jnp.bfloat16), "batch").astype(jnp.float32),
        lax.psum(group_grads[16].astype(jnp.bfloat16), "batch").astype(jnp.float32),
    )
    return (decoded[None], tokens_grad[None], skip_grad[None]) + tuple(total_grads)


def solution(mesh):
    in_specs = (
        P("batch", "seq", None),
        P("batch", "seq", None),
        P("batch", "seq", None),
        P("batch", None),
        P("seq"),
        P("seq"),
        P("seq", None),
        P("seq"),
        P("seq"),
        P("seq", None),
        P("seq"),
        P("seq"),
        P("seq"),
        P("seq", None),
        P("seq"),
        P("seq", None),
        P("seq"),
        P("seq", None),
        P("seq", None),
        P("seq", None),
        P("seq", None),
    )
    out_specs = (
        P("batch", "seq", None),
        P("batch", "seq", None),
        P("batch", "seq", None),
        P("seq"),
        P("seq"),
        P("seq", None),
        P("seq"),
        P("seq"),
        P("seq", None),
        P("seq"),
        P("seq"),
        P("seq"),
        P("seq", None),
        P("seq"),
        P("seq", None),
        P("seq"),
        P("seq", None),
        P("seq", None),
        P("seq", None),
        P("seq", None),
    )
    return jax.shard_map(
        on_device, mesh=mesh, in_specs=in_specs, out_specs=out_specs, check_vma=False
    )
```

profile of v0, /device:TPU:0, one launch (start us, length us, event | category | flops | bytes accessed | tf_op | source)
XLA Modules:
  0.0 956.3 jit_solution(15446312432970434500)
XLA Ops:
  16.7 26.0 %all-reduce.24 = (bf16[768]{0:T(1024)(128)(2,1)S(1)}, bf16[768]{0:T(1024)(128)(2,1)S(1)}, bf16[768]{0:T(1024)(128)(2,1)S(1)}, bf16[768]{0:T(1024)(128)(2,1)S(1)}...) all-reduce(bf16[768]{0:T(1024)(128)(2,1)S(1)} %dynamic-update-slice, ...), channel_id=1, replica_groups=mesh['batch'=4,'seq'=8] {'seq'}, use_global_device_ids=true, to_apply=%add.5 | all-reduce | flops 6144 | bytes 24576
  55.4 8.8 all-gather
  64.3 10.3 %all_gather.71 = bf16[3456,128]{1,0:T(8,128)(2,1)S(1)} all-gather(bf16[432,128]{1,0:T(8,128)(2,1)S(1)} %copy-done.61), channel_id=1, replica_groups=mesh['batch'=4,'seq'=8] {'seq'}, dimensions={0}, use_global_device_ids=true | all-gather | bytes 995328 | tf_op jit(solution)/shard_map/all_gather | solution.py:219
  74.6 11.1 %all_gather.72 = bf16[256,128]{1,0:T(8,128)(2,1)S(1)} all-gather(bf16[32,128]{1,0:T(8,128)(2,1)S(1)} %copy-done.74), channel_id=1, replica_groups=mesh['batch'=4,'seq'=8] {'seq'}, dimensions={0}, use_global_device_ids=true | all-gather | bytes 73728 | tf_op jit(solution)/shard_map/all_gather | solution.py:220
  103.4 5.9 all-gather.13.cloned.1.call-done
  111.2 38.7 %all-gather.15.cloned.1.call-done = bf16[768,3072]{1,0:T(8,128)(2,1)} async-done(((bf16[96,3072]{1,0:T(8,128)(2,1)}), bf16[768,3072]{1,0:T(8,128)(2,1)}) %all-gather.15.cloned.1.call-update) | async-done | bytes 4718608 | tf_op jit(solution)/shard_map/all_gather | solution.py:213
  150.0 8.4 multiply_convert_fusion.2
  158.4 32.3 %all-gather.17.cloned.1.call-done = bf16[3072,768]{1,0:T(8,128)(2,1)} async-done(((bf16[384,768]{1,0:T(8,128)(2,1)}), bf16[3072,768]{1,0:T(8,128)(2,1)}) %all-gather.17.cloned.1.call-update) | async-done | bytes 4718608 | tf_op jit(solution)/shard_map/all_gather | solution.py:215
  193.8 24.3 %all-gather.19.cloned.1.call-done = bf16[768,1024]{1,0:T(8,128)(2,1)} async-done(((bf16[96,1024]{1,0:T(8,128)(2,1)}), bf16[768,1024]{1,0:T(8,128)(2,1)}) %all-gather.19.cloned.1.call-update) | async-done | bytes 1572880 | tf_op jit(solution)/shard_map/all_gather | solution.py:217
  224.1 22.5 %all-gather.21.cloned.1.call-done = bf16[6912,128]{1,0:T(8,128)(2,1)} async-done(((bf16[864,128]{1,0:T(8,128)(2,1)}), bf16[6912,128]{1,0:T(8,128)(2,1)}) %all-gather.21.cloned.1.call-update) | async-done | bytes 1769488 | tf_op jit(solution)/shard_map/all_gather | solution.py:218
  261.8 13.1 %psum.175 = f32[4,128]{1,0:T(4,128)S(1)} all-reduce(f32[4,128]{1,0:T(4,128)S(1)} %fusion.100), channel_id=1, replica_groups=mesh['batch'=4,'seq'=8] {'seq'}, use_global_device_ids=true, to_apply=%region_10.11 | all-reduce | flops 512 | bytes 4096 | tf_op jit(solution)/shard_map/psum | solution.py:137
  275.8 11.8 %psum.176 = f32[4,128]{1,0:T(4,128)S(1)} all-reduce(f32[4,128]{1,0:T(4,128)S(1)} %fusion.66), channel_id=1, replica_groups=mesh['batch'=4,'seq'=8] {'seq'}, use_global_device_ids=true, to_apply=%region_11.12 | all-reduce | flops 512 | bytes 4096 | tf_op jit(solution)/shard_map/psum | solution.py:145
  307.6 12.9 %psum.177 = f32[4,128]{1,0:T(4,128)S(1)} all-reduce(f32[4,128]{1,0:T(4,128)S(1)} %fusion.98), channel_id=1, replica_groups=mesh['batch'=4,'seq'=8] {'seq'}, use_global_device_ids=true, to_apply=%region_12.13 | all-reduce | flops 512 | bytes 4096 | tf_op jit(solution)/shard_map/psum | solution.py:137
  321.4 13.3 %psum.178 = f32[4,128]{1,0:T(4,128)S(1)} all-reduce(f32[4,128]{1,0:T(4,128)S(1)} %fusion.59), channel_id=1, replica_groups=mesh['batch'=4,'seq'=8] {'seq'}, use_global_device_ids=true, to_apply=%region_13.14 | all-reduce | flops 512 | bytes 4096 | tf_op jit(solution)/shard_map/psum | solution.py:145
  339.3 11.8 %all-reduce.22 = (f32[4,128]{1,0:T(4,128)S(1)}, f32[4,128]{1,0:T(4,128)S(1)}) all-reduce(f32[4,128]{1,0:T(4,128)S(1)} %fusion.96, f32[4,128]{1,0:T(4,128)S(1)} %fusion.52), channel_id=1, replica_groups=mesh['batch'=4,'seq'=8] {'seq'}, use_global_device_ids=true, to_apply=%region_14.15 | all-reduce | flops 1024 | bytes 8192 | tf_op jit(solution)/shard_map/psum | solution.py:137
  365.6 15.5 %all-reduce.21 = (f32[4,128]{1,0:T(4,128)S(1)}, f32[4,128]{1,0:T(4,128)S(1)}) all-reduce(f32[4,128]{1,0:T(4,128)S(1)} %fusion.95, f32[4,128]{1,0:T(4,128)S(1)} %fusion.50), channel_id=1, replica_groups=mesh['batch'=4,'seq'=8] {'seq'}, use_global_device_ids=true, to_apply=%region_16.17 | all-reduce | flops 1024 | bytes 8192 | tf_op jit(solution)/shard_map/psum | solution.py:137
  397.5 5.8 fusion.169
  408.0 5.2 multiply_reduce_fusion
  432.0 3.9 convolution_convert_fusion.4
  435.9 4.2 convolution_convert_fusion.3
  458.6 14.8 %reduce-scatter.28.cloned.1.call-done = bf16[128,1536]{1,0:T(8,128)(2,1)} async-done(((bf16[1024,1536]{1,0:T(8,128)(2,1)}), bf16[128,1536]{1,0:T(8,128)(2,1)}) %reduce-scatter.28.cloned.1.call-update) | async-done | bytes 393232
  480.7 32.0 %reduce-scatter.24.cloned.1.call-done = bf16[432,128]{1,0:T(8,128)(2,1)} async-done(((bf16[3456,128]{1,0:T(8,128)(2,1)}), bf16[432,128]{1,0:T(8,128)(2,1)}) %reduce-scatter.24.cloned.1.call-update) | async-done | bytes 110608 | tf_op jit(solution)/shard_map/reduce_scatter | solution.py:495
  512.7 40.5 %reduce-scatter.14.cloned.1.call-done = bf16[96,768]{1,0:T(8,128)(2,1)} async-done(((bf16[768,768]{1,0:T(8,128)(2,1)}), bf16[96,768]{1,0:T(8,128)(2,1)}) %reduce-scatter.14.cloned.1.call-update) | async-done | bytes 147472 | tf_op jit(solution)/shard_map/reduce_scatter | solution.py:465
  553.2 42.1 %reduce-scatter.20.cloned.1.call-done = bf16[96,1024]{1,0:T(8,128)(2,1)} async-done(((bf16[768,1024]{1,0:T(8,128)(2,1)}), bf16[96,1024]{1,0:T(8,128)(2,1)}) %reduce-scatter.20.cloned.1.call-update) | async-done | bytes 196624 | tf_op jit(solution)/shard_map/reduce_scatter | solution.py:489
  595.4 43.0 %reduce-scatter.22.cloned.1.call-done = bf16[864,128]{1,0:T(8,128)(2,1)} async-done(((bf16[6912,128]{1,0:T(8,128)(2,1)}), bf16[864,128]{1,0:T(8,128)(2,1)}) %reduce-scatter.22.cloned.1.call-update) | async-done | bytes 221200 | tf_op jit(solution)/shard_map/reduce_scatter | solution.py:492
  638.4 57.7 %reduce-scatter.16.cloned.1.call-done = bf16[96,3072]{1,0:T(8,128)(2,1)} async-done(((bf16[768,3072]{1,0:T(8,128)(2,1)}), bf16[96,3072]{1,0:T(8,128)(2,1)}) %reduce-scatter.16.cloned.1.call-update) | async-done | bytes 589840 | tf_op jit(solution)/shard_map/reduce_scatter | solution.py:477
  696.1 57.2 %reduce-scatter.18.cloned.1.call-done = bf16[384,768]{1,0:T(8,128)(2,1)} async-done(((bf16[3072,768]{1,0:T(8,128)(2,1)}), bf16[384,768]{1,0:T(8,128)(2,1)}) %reduce-scatter.18.cloned.1.call-update) | async-done | bytes 589840 | tf_op jit(solution)/shard_map/reduce_scatter | solution.py:483
  753.4 51.9 %reduce-scatter.12.cloned.1.call-done = bf16[96,2304]{1,0:T(8,128)(2,1)} async-done(((bf16[768,2304]{1,0:T(8,128)(2,1)}), bf16[96,2304]{1,0:T(8,128)(2,1)}) %reduce-scatter.12.cloned.1.call-update) | async-done | bytes 442384 | tf_op jit(solution)/shard_map/reduce_scatter | solution.py:456
  812.0 23.1 %all-reduce.23 = (bf16[768]{0:T(1024)(128)(2,1)S(1)}, bf16[768]{0:T(1024)(128)(2,1)S(1)}, bf16[768]{0:T(1024)(128)(2,1)S(1)}, bf16[768]{0:T(1024)(128)(2,1)S(1)}...) all-reduce(bf16[768]{0:T(1024)(128)(2,1)S(1)} %get-tuple-element.22, ...), channel_id=3, replica_groups=mesh['batch'=4,'seq'=8] {'seq'}, use_global_device_ids=true, to_apply=%region_25.26.clone | all-reduce | flops 9216 | bytes 36864
  835.8 6.4 reduce-scatter.26.cloned.1.call-done
  842.1 19.2 %all-reduce.25 = (bf16[96]{0:T(256)(128)(2,1)S(1)}, bf16[96]{0:T(256)(128)(2,1)S(1)}, bf16[96]{0:T(256)(128)(2,1)S(1)}, bf16[96]{0:T(256)(128)(2,1)S(1)}, bf16[9...) all-reduce(bf16[96]{0:T(256)(128)(2,1)S(1)} %dynamic-slice.9, ...), channel_id=1, replica_groups=mesh['batch'=4,'seq'=8] {'batch'}, use_global_device_ids=true, to_apply=%region_26.27 | all-reduce | flops 5248 | bytes 20992 | tf_op jit(solution)/shard_map/psum | solution.py:503
  867.6 73.6 %all-reduce.29.cloned.1.call-done = (bf16[96,2304]{1,0:T(8,128)(2,1)}, bf16[96,768]{1,0:T(8,128)(2,1)}, bf16[96,3072]{1,0:T(8,128)(2,1)}, bf16[384,768]{1,0:T(8,...) async-done(((bf16[96,2304]{1,0:T(8,128)(2,1)}, bf16[96,768]{1,0:T(8,128)(2,1)}, bf16[96,3072]{1,0:T(8,128)(2,1)}, ...) | async-done | bytes 2297872 | tf_op jit(solution)/shard_map/psum | solution.py:505
  (522 shorter events, 190.6 us)
Async XLA Ops:
  7.2 39.6 %all-gather.9.cloned.1.call-start = ((), (), s32[]{:S(2)}) async-start(), calls=%async_computation.9 | async-start | bytes 3981312 | tf_op jit(solution)/shard_map/all_gather | solution.py:206
  7.9 81.0 %all-gather.11.cloned.1.call-start = ((), (), s32[]{:S(2)}) async-start(), calls=%async_computation.10 | async-start | bytes 3538944 | tf_op jit(solution)/shard_map/all_gather | solution.py:276
  50.6 58.7 %all-gather.13.cloned.1.call-start = ((), (), s32[]{:S(2)}) async-start(), calls=%async_computation.11 | async-start | bytes 1327104 | tf_op jit(solution)/shard_map/all_gather | solution.py:209
  51.3 98.6 %all-gather.15.cloned.1.call-start = ((), (), s32[]{:S(2)}) async-start(), calls=%async_computation.12 | async-start | bytes 5308416 | tf_op jit(solution)/shard_map/all_gather | solution.py:213
  51.9 138.8 %all-gather.17.cloned.1.call-start = ((), (), s32[]{:S(2)}) async-start(), calls=%async_computation.13 | async-start | bytes 5308416 | tf_op jit(solution)/shard_map/all_gather | solution.py:215
  52.5 165.7 %all-gather.19.cloned.1.call-start = ((), (), s32[]{:S(2)}) async-start(), calls=%async_computation.14 | async-start | bytes 1769472 | tf_op jit(solution)/shard_map/all_gather | solution.py:217
  53.1 193.5 %all-gather.21.cloned.1.call-start = ((), (), s32[]{:S(2)}) async-start(), calls=%async_computation.15 | async-start | bytes 1990656 | tf_op jit(solution)/shard_map/all_gather | solution.py:218
  53.8 419.6 %reduce-scatter.28.cloned.1.call-start = ((), (), s32[]{:S(2)}) async-start(), calls=%async_computation.24 | async-start | bytes 3538944
  111.0 294.7 %copy-start.63 = (f32[128]{0:T(128)}, f32[128]{0:T(128)S(1)}, u32[]{:S(2)}) copy-start(f32[128]{0:T(128)S(1)} %broadcast_multiply_fusion.4) | copy-start | bytes 1540
  193.8 55.7 %copy-start.45 = (bf16[128,768]{1,0:T(8,128)(2,1)}, bf16[128,768]{1,0:T(8,128)(2,1)S(1)}, u32[]{:S(2)}) copy-start(bf16[128,768]{1,0:T(8,128)(2,1)S(1)} %fusion.35) | copy-start | bytes 589828
  220.4 115.0 %copy-start.21 = (bf16[8,4,4,2,2,2,128]{6,5,2,4,1,3,0:T(2,128)(2,1)}, bf16[8,4,4,2,2,2,128]{6,5,2,4,1,3,0:T(2,128)(2,1)S(1)}, u32[]{:S(2)}) copy-start(bf16[8,4,4,2,2,2,128]{6,5,2,4,1,3,0:T(2,128)(2,1)S(1)} %copy.83) | copy-start | bytes 786436
  220.4 29.1 %collective-permute-start = (bf16[1,8,8,256]{3,2,1,0:T(8,128)(2,1)S(1)}, bf16[1,8,8,256]{3,2,1,0:T(8,128)(2,1)S(1)}, u32[]{:S(2)}, u32[]{:S(2)}) collective-permute-start(bf16[1,8,8,256]{3,2,1,0:T(8,128)(2,1)S(1)} %get-tuple-element.124), channel_id=1, source_target_pairs={{0,1},{1,2},{2,3},{3,4},{4,5},{5,6},{6,7},{8,9},{9,10},{10,11},{11... | collective-permute-start | bytes 98312 | tf_op jit(solution)/shard_map/ppermute | solution.py:26
  222.6 26.9 %collective-permute-start.1 = (bf16[1,8,8,256]{3,2,1,0:T(8,128)(2,1)S(1)}, bf16[1,8,8,256]{3,2,1,0:T(8,128)(2,1)S(1)}, u32[]{:S(2)}, u32[]{:S(2)}) collective-permute-start(bf16[1,8,8,256]{3,2,1,0:T(8,128)(2,1)S(1)} %get-tuple-element.125), channel_id=1, source_target_pairs={{1,0},{2,1},{3,2},{4,3},{5,4},{6,5},{7,6},{9,8},{10,9},{11,10},{12... | collective-permute-start | bytes 98312 | tf_op jit(solution)/shard_map/ppermute | solution.py:28
  290.1 9.9 %collective-permute-start.2 = (bf16[1,8,8,128]{3,2,1,0:T(8,128)(2,1)S(1)}, bf16[1,8,8,128]{3,2,1,0:T(8,128)(2,1)S(1)}, u32[]{:S(2)}, u32[]{:S(2)}) collective-permute-start(bf16[1,8,8,128]{3,2,1,0:T(8,128)(2,1)S(1)} %get-tuple-element.131), channel_id=1, source_target_pairs={{0,1},{1,2},{2,3},{3,4},{4,5},{5,6},{6,7},{8,9},{9,10},{10,11},{11... | collective-permute-start | bytes 49160 | tf_op jit(solution)/shard_map/ppermute | solution.py:26
  291.9 8.2 collective-permute-start.3
  352.4 3.3 collective-permute-start.4
  354.2 3.1 collective-permute-start.5
  382.3 3.2 collective-permute-start.6
  383.7 4.9 collective-permute-start.7
  421.5 91.2 %reduce-scatter.24.cloned.1.call-start = ((), (), s32[]{:S(2)}) async-start(), calls=%async_computation.22 | async-start | bytes 995328 | tf_op jit(solution)/shard_map/reduce_scatter | solution.py:495
  428.3 124.9 %reduce-scatter.14.cloned.1.call-start = ((), (), s32[]{:S(2)}) async-start(), calls=%async_computation.17 | async-start | bytes 1327104 | tf_op jit(solution)/shard_map/reduce_scatter | solution.py:465
  430.1 165.2 %reduce-scatter.20.cloned.1.call-start = ((), (), s32[]{:S(2)}) async-start(), calls=%async_computation.20 | async-start | bytes 1769472 | tf_op jit(solution)/shard_map/reduce_scatter | solution.py:489
  432.0 206.4 %reduce-scatter.22.cloned.1.call-start = ((), (), s32[]{:S(2)}) async-start(), calls=%async_computation.21 | async-start | bytes 1990656 | tf_op jit(solution)/shard_map/reduce_scatter | solution.py:492
  445.3 250.8 %reduce-scatter.16.cloned.1.call-start = ((), (), s32[]{:S(2)}) async-start(), calls=%async_computation.18 | async-start | bytes 5308416 | tf_op jit(solution)/shard_map/reduce_scatter | solution.py:477
  449.1 304.2 %reduce-scatter.18.cloned.1.call-start = ((), (), s32[]{:S(2)}) async-start(), calls=%async_computation.19 | async-start | bytes 5308416 | tf_op jit(solution)/shard_map/reduce_scatter | solution.py:483
  454.0 351.2 %reduce-scatter.12.cloned.1.call-start = ((), (), s32[]{:S(2)}) async-start(), calls=%async_computation.16 | async-start | bytes 3981312 | tf_op jit(solution)/shard_map/reduce_scatter | solution.py:456
  478.5 328.0 %copy-start.53 = (f32[1024,128]{1,0:T(8,128)S(1)}, f32[1024,128]{1,0:T(8,128)}, u32[]{:S(2)}) copy-start(f32[1024,128]{1,0:T(8,128)} %get-tuple-element.69) | copy-start | bytes 1572868
  478.5 328.9 %copy-start.20 = (f32[1024,256]{1,0:T(8,128)S(1)}, f32[1024,256]{1,0:T(8,128)}, u32[]{:S(2)}) copy-start(f32[1024,256]{1,0:T(8,128)} %copy-done.19) | copy-start | bytes 3145732
  478.6 363.6 %reduce-scatter.26.cloned.1.call-start = ((), (), s32[]{:S(2)}) async-start(), calls=%async_computation.23 | async-start | bytes 73728 | tf_op jit(solution)/shard_map/reduce_scatter | solution.py:498
  480.7 325.9 %copy-start.54 = (f32[1024,128]{1,0:T(8,128)S(1)}, f32[1024,128]{1,0:T(8,128)}, u32[]{:S(2)}) copy-start(f32[1024,128]{1,0:T(8,128)} %get-tuple-element.145) | copy-start | bytes 1572868
  480.7 460.5 %all-reduce.29.cloned.1.call-start = ((), (), s32[]{:S(2)}) async-start(), calls=%async_computation.25 | async-start | bytes 4595712 | tf_op jit(solution)/shard_map/psum | solution.py:505
  808.5 58.2 %copy-start.25 = (f32[128,768]{1,0:T(8,128)S(1)}, f32[128,768]{1,0:T(8,128)}, u32[]{:S(2)}) copy-start(f32[128,768]{1,0:T(8,128)} %copy-done.23) | copy-start | bytes 1179652
  (80 other events, 536.8 us)
Sparse Core Ops, SparseCore 0:
  9.9 36.8 all-gather.8
  50.7 32.5 all-gather.10
  85.2 24.0 all-gather.12
  111.0 38.9 all-gather.14
  151.7 38.9 all-gather.16
  192.4 25.7 all-gather.18
  220.0 26.5 all-gather.20
  421.6 51.8 reduce-scatter.27
  477.6 35.0 reduce-scatter.23
  516.4 36.7 reduce-scatter.13
  556.9 38.4 reduce-scatter.19
  598.9 39.3 reduce-scatter.21
  642.2 53.8 reduce-scatter.15
  699.4 53.8 reduce-scatter.17
  757.1 48.0 reduce-scatter.11
  808.9 33.1 reduce-scatter.25
  844.9 96.1 all-reduce.28
where the time goes:
time: 962 us; the launch traced here: 956 us
  waiting for transfers between devices  553 us (57%)
  blocking collectives  177 us (18%)
  matrix products  98.6 us (10%)
  local copies, waits for them, and re-layouts  65.5 us (7%)
  other arithmetic  29.5 us (3%)
  between operations  18.4 us (2%)
  starting transfers between devices  14.1 us (1%)
    psum x1, waiting for transfers between devices, on_device(): lax.psum(group_grads[2].astype(jnp.bfloat16), 'batch').astype(jnp.float32)  73.6 us
    reduce_scatter x1, waiting for transfers between devices, on_device(): lax.psum_scatter(partial_grads[9].astype(jnp.bfloat16), 'seq', scatter_di...  57.7 us
    reduce_scatter x1, waiting for transfers between devices, on_device(): lax.psum_scatter(partial_grads[11].astype(jnp.bfloat16), 'seq', scatter_d...  57.2 us
    psum x4, blocking collectives, crop_total(): return lax.psum(values, 'seq')  53.3 us
    reduce_scatter x1, waiting for transfers between devices, on_device(): lax.psum_scatter(partial_grads[2].astype(jnp.bfloat16), 'seq', scatter_di...  51.9 us
    unnamed x2, blocking collectives  49.1 us
    reduce_scatter x1, waiting for transfers between devices, on_device(): lax.psum_scatter(partial_grads[14].astype(jnp.bfloat16), 'seq', scatter_d...  43 us
    reduce_scatter x1, waiting for transfers between devices, on_device(): lax.psum_scatter(partial_grads[13].astype(jnp.bfloat16), 'seq', scatter_d...  42.1 us
  transfers between devices with their start and end apart: 25, of which 18 were waited for; matrix products, arithmetic and copies ran while one was open for 11% of the time, Pallas kernels for 0%

commit v1 on v0

v1 whole, which is shorter than its diff:
```python
import math

import jax
import jax.numpy as jnp
from jax import lax
from jax.sharding import PartitionSpec as P

HEADS = 12
PH = 4
CROPS = 4


PRECISE = lax.Precision.HIGHEST
EPS_LAYER = 1e-06
EPS_CROP = 1e-05
BF = jnp.bfloat16
F32 = jnp.float32


def exact_dot(first_arg, second_arg):
    return jnp.dot(first_arg, second_arg, precision=PRECISE)


def bf_dot(first_arg, second_arg):
    return jnp.dot(first_arg, second_arg, preferred_element_type=F32)


def cross_dot(first_arg, second_arg):
    return lax.dot_general(
        first_arg, second_arg, (((0,), (0,)), ((), ())), preferred_element_type=F32
    )


def back_dot(first_arg, second_arg):
    return lax.dot_general(
        first_arg, second_arg, (((1,), (1,)), ((), ())), preferred_element_type=F32
    )


def spread_rows(member, per_crop):
    return lax.dot_general(member, per_crop, (((0,), (0,)), ((), ())), precision=PRECISE)


def crops_of(lengths, indices):
    crop_ends = jnp.cumsum(lengths)
    return jnp.sum((indices[:, None] >= crop_ends[None, :]).astype(jnp.int32), axis=1)


def layer_norm(values, gain_vec, shift_vec):
    average = jnp.mean(values, axis=-1, keepdims=True)
    centred = values - average
    inv_std = lax.rsqrt(jnp.mean(centred * centred, axis=-1, keepdims=True) + EPS_LAYER)
    unit_rows = centred * inv_std
    return (unit_rows * gain_vec + shift_vec, unit_rows, inv_std)


def layer_back(upstream, unit_rows, inv_std, gain_vec):
    scaled = upstream * gain_vec
    return inv_std * (
        scaled
        - jnp.mean(scaled, axis=-1, keepdims=True)
        - unit_rows * jnp.mean(scaled * unit_rows, axis=-1, keepdims=True)
    )


def gelu_exact(values):
    return jax.nn.gelu(values, approximate=False)


def gelu_back(values, upstream):
    return jax.vjp(gelu_exact, values)[1](upstream)[0]


def swap(values, axis, mask):
    count = lax.axis_size(axis)
    return lax.ppermute(values, axis, [(i, i ^ mask) for i in range(count)])


def gather_rel(values, axis, stride, count):
    return jnp.stack([values] + [swap(values, axis, m * stride) for m in range(1, count)])


def pick(blocks, index):
    return lax.dynamic_index_in_dim(blocks, index, 0, keepdims=False)


def unxor(blocks, index):
    count = blocks.shape[0]
    bits = count.bit_length() - 1
    tail = blocks.shape[1:]
    cube = blocks.reshape((2,) * bits + tail)
    for bit in range(bits):
        dim = bits - 1 - bit
        cube = jnp.where(((index >> bit) & 1) == 1, jnp.flip(cube, dim), cube)
    return cube.reshape(blocks.shape)


def deal_rel(blocks, axis, stride, index):
    count = blocks.shape[0]
    return [pick(blocks, index)] + [
        swap(pick(blocks, index ^ m), axis, m * stride) for m in range(1, count)
    ]


def sum_list(parts):
    total = parts[0].astype(F32)
    for part in parts[1:]:
        total = total + part.astype(F32)
    return total


def batch_sum(values):
    count = lax.axis_size("batch")
    if count == 1:
        return values.astype(F32)
    index = lax.axis_index("batch")
    rows = values.shape[0]
    piece = -(-rows // count)
    if piece * count > rows:
        values = jnp.pad(values, ((0, piece * count - rows), (0, 0)))
    pieces = values.reshape((count, piece) + values.shape[1:])
    own = sum_list(deal_rel(pieces, "batch", 1, index)).astype(BF)
    total = unxor(gather_rel(own, "batch", 1, count), index)
    return total.reshape(values.shape)[:rows].astype(F32)


def with_rims(grid_field):
    count = lax.axis_size("seq")
    ends = count - 1
    head = grid_field[:1]
    tail = grid_field[-1:]
    extended = jnp.concatenate(
        [
            lax.ppermute(tail, "seq", [(i, (i + 1) % count) for i in range(ends)]),
            grid_field,
            lax.ppermute(head, "seq", [((i + 1) % count, i) for i in range(ends)]),
        ],
        axis=0,
    )
    return jnp.pad(extended, ((0, 0), (1, 1), (1, 1), (0, 0)))


def planes(padded, keep_mask, layer_idx):
    depth_rows = keep_mask.shape[0]
    grid_high = padded.shape[1] - 2
    grid_wide = padded.shape[2] - 2
    slab_rows = padded[layer_idx : layer_idx + depth_rows] * keep_mask[:, None, None, None]
    pieces = [
        slab_rows[:, row_off : row_off + grid_high, col_off : col_off + grid_wide, :]
        for row_off in range(3)
        for col_off in range(3)
    ]
    return jnp.concatenate(pieces, axis=-1).reshape(depth_rows * grid_high * grid_wide, -1)


def forward_taps(weight):
    block_len = weight.shape[0] // 3
    return [weight[layer_idx * block_len : (layer_idx + 1) * block_len] for layer_idx in range(3)]


def backward_taps(weight, in_chans):
    cube = weight.reshape(3, 3, 3, in_chans, weight.shape[1])[::-1, ::-1, ::-1]
    turned = jnp.swapaxes(cube, 3, 4)
    return [turned[layer_idx].reshape(9 * weight.shape[1], in_chans) for layer_idx in range(3)]


def stencil(padded, keep_masks, matrices):
    running = None
    for layer_idx in range(3):
        term = bf_dot(planes(padded, keep_masks[layer_idx], layer_idx), matrices[layer_idx])
        running = term if running is None else running + term
    return running


def weight_grad(padded, keep_masks, upstream):
    return jnp.concatenate(
        [
            cross_dot(planes(padded, keep_masks[layer_idx], layer_idx), upstream)
            for layer_idx in range(3)
        ],
        axis=0,
    )


def on_device(
    tokens,
    skip_features,
    out_grad,
    crop_lengths,
    attend_gain,
    attend_shift,
    joint_weight,
    query_bias,
    value_bias,
    output_weight,
    output_bias,
    mixer_gain,
    mixer_shift,
    expand_weight,
    expand_bias,
    reduce_weight,
    reduce_bias,
    upsample_weight,
    kernel_first,
    kernel_second,
    residual_weight,
):
    count = lax.axis_size("seq")
    high = math.gcd(HEADS, count)
    low = count // high
    seq_index = lax.axis_index("seq")
    hi = seq_index // low
    lo = seq_index % low
    width = tokens.shape[2]
    shard = joint_weight.shape[0]
    head_dim = width // HEADS
    heads = HEADS // high
    span = heads * head_dim
    hidden = expand_weight.shape[1]
    hid_span = hidden // high
    hid_shard = hidden // count
    channels = residual_weight.shape[1]
    score_scale = 1.0 / math.sqrt(head_dim)
    plane_size = PH * PH
    tok_rows = tokens.shape[1]
    rows = high * tok_rows
    slices = tok_rows // plane_size
    depth_rows = 2 * slices
    positions = depth_rows * 4 * plane_size
    lengths = crop_lengths[0]

    def plane_gather(values):
        return gather_rel(values, "seq", low, high)

    def plane_deal(blocks):
        return deal_rel(blocks, "seq", low, hi)

    def chip_gather(values):
        return gather_rel(values, "seq", 1, low)

    def chip_sum(blocks):
        return sum_list(deal_rel(blocks, "seq", 1, lo)).astype(BF)

    def plane_sum(blocks):
        return sum_list(
            [blocks[0]] + [swap(blocks[m].astype(BF), "seq", m * low) for m in range(1, high)]
        )

    def all_gather(values):
        return lax.all_gather(values, "seq", axis=0, tiled=True)

    def owners(rel_hi, rel_lo):
        return (hi ^ rel_hi) * low + (lo ^ rel_lo)

    gathered_tokens = plane_gather(tokens[0]).reshape(rows, width)
    vec_own = jnp.concatenate(
        [
            jnp.stack(
                [
                    attend_gain,
                    attend_shift,
                    query_bias,
                    value_bias,
                    output_bias,
                    mixer_gain,
                    mixer_shift,
                    reduce_bias,
                ]
            ),
            expand_bias.reshape(hid_shard // shard, shard),
        ],
        axis=0,
    )
    vec_rel = chip_gather(plane_gather(vec_own))
    vec_abs = unxor(jnp.swapaxes(unxor(vec_rel, lo), 0, 1), hi).reshape(count, -1, shard)
    vecs = vec_abs.astype(F32).transpose(1, 0, 2)
    flat = vecs[:8].reshape(8, width)
    gain_a, shift_a, query_b, value_b, out_b, gain_m, shift_m, reduce_b = [
        flat[j] for j in range(8)
    ]
    expand_b = vec_abs[:, 8:].astype(F32).reshape(hidden)

    def own_span(vector, length):
        return lax.dynamic_slice_in_dim(vector, hi * length, length)

    def columns_for(weight, parts):
        per = weight.shape[1] // (parts * high)
        cut = weight.reshape(shard, parts, high, per).transpose(2, 0, 1, 3)
        cut = cut.reshape(high, shard, parts * per)
        rel = chip_gather(jnp.stack(plane_deal(cut)))
        natural = unxor(jnp.swapaxes(unxor(rel, lo), 0, 1), hi)
        return natural.reshape(width, parts * per)

    joint_w = columns_for(joint_weight, 3)
    out_rel = unxor(chip_gather(plane_gather(output_weight)), lo)
    out_w = jnp.swapaxes(out_rel, 0, 1).reshape(width, width)
    expand_w = columns_for(expand_weight, 1)
    reduce_w = unxor(chip_gather(reduce_weight), lo).reshape(hid_span, width)
    upsample_w = all_gather(upsample_weight)
    conv_shards = jnp.concatenate([kernel_first, kernel_second, residual_weight], axis=0)
    conv_all = lax.all_gather(conv_shards, "seq", axis=0)
    cut_one = kernel_first.shape[0]
    cut_two = cut_one + kernel_second.shape[0]
    kernel_one = conv_all[:, :cut_one].reshape(-1, channels)
    kernel_two = conv_all[:, cut_one:cut_two].reshape(-1, channels)
    residual_w = conv_all[:, cut_two:].reshape(-1, channels)

    def token_crops(rel_lo):
        starts = jnp.stack([owners(m, rel_lo) for m in range(high)]) * slices
        ids = starts[:, None] + jnp.arange(slices, dtype=jnp.int32)[None, :]
        return jnp.repeat(crops_of(lengths, ids.reshape(-1)), plane_size)

    own_crop = token_crops(0)
    all_crop = jnp.concatenate([token_crops(s) for s in range(low)])
    same_crop = (own_crop[:, None] == all_crop[None, :])[None]

    def split_heads(row_block):
        return row_block.reshape(row_block.shape[0], heads, head_dim)

    normed_a, unit_a, inv_a = layer_norm(gathered_tokens.astype(F32), gain_a, shift_a)
    normed_low = normed_a.astype(BF)
    joint_out = bf_dot(normed_low, joint_w)
    queries = (joint_out[:, :span] + own_span(query_b, span)).astype(BF)
    key_rows = joint_out[:, span : 2 * span].astype(BF)
    value_rows = (joint_out[:, 2 * span :] + own_span(value_b, span)).astype(BF)
    kv_all = chip_gather(jnp.concatenate([key_rows, value_rows], axis=1))
    kv_all = kv_all.reshape(low * rows, 2 * span)
    key_heads = split_heads(kv_all[:, :span])
    value_heads = split_heads(kv_all[:, span:])
    query_heads = split_heads(queries)
    scores = (
        jnp.einsum("the,lhe->htl", query_heads, key_heads, preferred_element_type=F32)
        * score_scale
    )
    masked = jnp.where(same_crop, scores, -1000000000.0)
    highest = jnp.max(masked, axis=-1, keepdims=True)
    exp_scores = jnp.exp(masked - highest)
    totals = jnp.sum(exp_scores, axis=-1, keepdims=True)
    log_total = highest + jnp.log(totals)
    probability = (exp_scores / totals).astype(BF)
    attended = (
        jnp.einsum("htl,lhe->the", probability, value_heads, preferred_element_type=F32)
        .reshape(rows, span)
        .astype(BF)
    )
    att_blocks = attended.reshape(high, tok_rows, span)
    att_rel = [att_blocks[0]] + [swap(att_blocks[m], "seq", m * low) for m in range(1, high)]
    inputs = tokens[0].astype(F32)
    middle = inputs + bf_dot(jnp.concatenate(att_rel, axis=1), out_w) + out_b
    normed_m, unit_m, inv_m = layer_norm(middle, gain_m, shift_m)
    inner_low = plane_gather(normed_m.astype(BF)).reshape(rows, width)
    expanded = bf_dot(inner_low, expand_w) + own_span(expand_b, hid_span)
    activated = gelu_exact(expanded).astype(BF)
    mixed_part = bf_dot(activated, reduce_w).reshape(high, tok_rows, width)
    encoded = (middle + plane_sum(mixed_part) + reduce_b).astype(BF)
    up_rows = bf_dot(encoded, upsample_w).reshape(slices, PH, PH, 2, 2, 2, channels)
    upsampled = (
        up_rows.transpose(0, 3, 1, 4, 2, 5, 6)
        .reshape(depth_rows, 2 * PH, 2 * PH, channels)
        .astype(BF)
    )

    joined = jnp.concatenate(
        [upsampled, skip_features[0].reshape(depth_rows, 2 * PH, 2 * PH, channels)], axis=-1
    )
    up_index = seq_index * depth_rows - 1 + jnp.arange(depth_rows + 2, dtype=jnp.int32)
    up_crop = crops_of(lengths, up_index // 2)
    keep_masks = [
        (up_crop[layer_idx : layer_idx + depth_rows] == up_crop[1 : 1 + depth_rows]).astype(BF)
        for layer_idx in range(3)
    ]
    pos_crop = jnp.repeat(up_crop[1 : 1 + depth_rows], 4 * plane_size)
    member = (jnp.arange(CROPS, dtype=jnp.int32)[:, None] == pos_crop[None, :]).astype(F32)
    counts = (lengths * 8 * plane_size).astype(F32)[:, None]

    crop_ends = jnp.cumsum(lengths)
    dev_rel = jnp.stack([owners(m, s) for s in range(low) for m in range(high)])
    first = (dev_rel * slices)[:, None]
    shared = jnp.minimum(crop_ends[None], first + slices) - jnp.maximum(
        (crop_ends - lengths)[None], first
    )
    dev_counts = (jnp.maximum(shared, 0) * 8 * plane_size).astype(F32)[:, :, None]
    own_counts = dev_counts[0]

    def stat_gather(first_part, second_part):
        pair = jnp.concatenate([first_part, second_part], axis=0)
        return chip_gather(plane_gather(pair)).reshape(count, 2, CROPS, -1)

    def crop_norm(values):
        local_sum = exact_dot(member, values)
        local_mean = local_sum / jnp.maximum(own_counts, 1.0)
        about = values - spread_rows(member, local_mean)
        local_dev = exact_dot(member, about * about)
        both = stat_gather(local_sum, local_dev)
        average = jnp.sum(both[:, 0], axis=0) / counts
        off = both[:, 0] / jnp.maximum(dev_counts, 1.0) - average
        spread = jnp.sum(both[:, 1] + dev_counts * off * off, axis=0) / counts
        inv_rows = spread_rows(member, lax.rsqrt(spread + EPS_CROP))
        return ((values - spread_rows(member, average)) * inv_rows, inv_rows)

    def crop_backnorm(upstream, unit_rows, inv_rows):
        both = stat_gather(exact_dot(member, upstream), exact_dot(member, upstream * unit_rows))
        sums = jnp.sum(both, axis=0) / counts
        return inv_rows * (
            upstream - spread_rows(member, sums[0]) - unit_rows * spread_rows(member, sums[1])
        )

    joined_rim = with_rims(joined)
    first_conv = stencil(joined_rim, keep_masks, forward_taps(kernel_one))
    first_unit, first_inv = crop_norm(first_conv)
    act_one = gelu_exact(first_unit).astype(BF)
    act_rim = with_rims(act_one.reshape(depth_rows, 2 * PH, 2 * PH, channels))
    second_conv = stencil(act_rim, keep_masks, forward_taps(kernel_two))
    second_unit, second_inv = crop_norm(second_conv)
    joined_rows = joined.reshape(positions, 2 * channels)
    summed = second_unit + bf_dot(joined_rows, residual_w)
    decoded = gelu_exact(summed).astype(BF)
    grad_summed = gelu_back(summed, out_grad[0].astype(F32))
    grad_resid = grad_summed.astype(BF)
    grad_second = crop_backnorm(grad_summed, second_unit, second_inv).astype(BF)
    residual_grad = cross_dot(joined_rows, grad_resid)
    second_rim = with_rims(grad_second.reshape(depth_rows, 2 * PH, 2 * PH, channels))
    kernel_two_grad = weight_grad(act_rim, keep_masks, grad_second)
    grad_act = stencil(second_rim, keep_masks, backward_taps(kernel_two, channels))
    grad_first = crop_backnorm(gelu_back(first_unit, grad_act), first_unit, first_inv).astype(BF)
    kernel_one_grad = weight_grad(joined_rim, keep_masks, grad_first)
    first_rim = with_rims(grad_first.reshape(depth_rows, 2 * PH, 2 * PH, channels))
    grad_joined = stencil(
        first_rim, keep_masks, backward_taps(kernel_one, 2 * channels)
    ) + back_dot(grad_resid, residual_w)
    skip_grad = grad_joined[:, channels:]
    grad_up = grad_joined[:, :channels].astype(BF).reshape(slices, 2, PH, 2, PH, 2, channels)
    grad_up_rows = grad_up.transpose(0, 2, 4, 1, 3, 5, 6).reshape(tok_rows, 8 * channels)

    def shard_sum(partial):
        blocks = partial.astype(BF).reshape((high, low, -1) + partial.shape[1:])
        own = chip_sum(jnp.swapaxes(blocks, 0, 1))
        return sum_list(plane_deal(own)).astype(BF)

    conv_part = jnp.concatenate(
        [
            kernel_one_grad.astype(BF).reshape(count, -1, channels),
            kernel_two_grad.astype(BF).reshape(count, -1, channels),
            residual_grad.astype(BF).reshape(count, -1, channels),
        ],
        axis=1,
    )
    conv_sum = batch_sum(shard_sum(conv_part.reshape(-1, channels)))
    upsample_grad = batch_sum(shard_sum(cross_dot(encoded, grad_up_rows)))
    grad_encoded = back_dot(grad_up_rows, upsample_w)
    own_mixed = grad_encoded.astype(BF)
    grad_mixed = plane_gather(own_mixed).reshape(rows, width)
    reduce_bias_grad = jnp.sum(own_mixed.astype(F32), axis=0)
    reduce_part = cross_dot(activated, grad_mixed).astype(BF).reshape(low, hid_shard, width)
    reduce_grad = batch_sum(chip_sum(reduce_part))
    grad_expanded = gelu_back(expanded, back_dot(grad_mixed, reduce_w)).astype(BF)

    def column_grad(partial, parts):
        blocks = partial.astype(BF).reshape(high, low, shard, -1)
        own = chip_sum(jnp.swapaxes(blocks, 0, 1))
        cols = unxor(jnp.stack(plane_deal(own)), hi)
        cols = cols.reshape(high, shard, parts, -1).transpose(1, 2, 0, 3)
        return cols.reshape(shard, -1)

    expand_grad = batch_sum(column_grad(cross_dot(inner_low, grad_expanded), 1))
    expand_bias_part = jnp.sum(grad_expanded.astype(F32), axis=0).astype(BF)
    inner_part = back_dot(grad_expanded, expand_w).reshape(high, tok_rows, width)
    grad_inner = plane_sum(inner_part)
    mixer_gain_grad = jnp.sum(grad_inner * unit_m, axis=0)
    mixer_shift_grad = jnp.sum(grad_inner, axis=0)
    grad_middle = grad_encoded + layer_back(grad_inner, unit_m, inv_m, gain_m)
    own_branch = grad_middle.astype(BF)
    grad_branch = plane_gather(own_branch).reshape(rows, width)
    output_bias_grad = jnp.sum(own_branch.astype(F32), axis=0)
    output_part = cross_dot(attended, grad_branch).astype(BF).reshape(low, shard, width)
    output_grad = batch_sum(chip_sum(output_part))
    own_out_w = out_w[:span]
    grad_attended = back_dot(grad_branch, own_out_w).astype(BF)
    again_scores = (
        jnp.einsum("the,lhe->htl", query_heads, key_heads, preferred_element_type=F32)
        * score_scale
    )
    again_prob = jnp.exp(jnp.where(same_crop, again_scores, -1000000000.0) - log_total)
    attended_heads = split_heads(grad_attended)
    grad_weights = jnp.einsum(
        "the,lhe->htl", attended_heads, value_heads, preferred_element_type=F32
    )
    inner_sum = jnp.sum(again_prob * grad_weights, axis=-1, keepdims=True)
    grad_scores = (again_prob * (grad_weights - inner_sum)).astype(BF)
    grad_queries = (
        (
            jnp.einsum("htl,lhe->the", grad_scores, key_heads, preferred_element_type=F32)
            * score_scale
        )
        .reshape(rows, span)
        .astype(BF)
    )
    prob_low = again_prob.astype(BF)
    key_part = (
        jnp.einsum("htl,the->lhe", grad_scores, query_heads, preferred_element_type=F32)
        * score_scale
    )
    value_part = jnp.einsum("htl,the->lhe", prob_low, attended_heads, preferred_element_type=F32)
    kv_part = jnp.concatenate(
        [key_part.reshape(low, rows, span), value_part.reshape(low, rows, span)], axis=2
    )
    kv_grad = sum_list(
        [kv_part[0]] + [swap(kv_part[s].astype(BF), "seq", s) for s in range(1, low)]
    ).astype(BF)
    grad_joint = jnp.concatenate([grad_queries, kv_grad], axis=1)
    joint_part = column_grad(cross_dot(normed_low, grad_joint), 3)
    joint_grad = batch_sum(joint_part)
    normed_part = back_dot(grad_joint, joint_w)
    attend_gain_grad = jnp.sum(normed_part * unit_a, axis=0)
    attend_shift_grad = jnp.sum(normed_part, axis=0)
    grad_normed = plane_sum(normed_part.reshape(high, tok_rows, width))
    tokens_grad = grad_middle + layer_back(grad_normed, unit_a[:tok_rows], inv_a[:tok_rows], gain_a)

    joint_bias = jnp.sum(grad_joint.astype(F32), axis=0)
    whole = jnp.stack(
        [
            attend_gain_grad,
            attend_shift_grad,
            output_bias_grad,
            mixer_gain_grad,
            mixer_shift_grad,
            reduce_bias_grad,
        ]
    )
    whole = whole.astype(BF).reshape(6, count, shard).transpose(1, 0, 2).reshape(count, -1)
    whole = sum_list(
        plane_deal(chip_sum(jnp.swapaxes(whole.reshape(high, low, -1), 0, 1)))
    ).astype(BF)
    part = chip_sum(
        jnp.concatenate(
            [
                joint_bias[:span].astype(BF).reshape(low, shard),
                joint_bias[2 * span :].astype(BF).reshape(low, shard),
                expand_bias_part.reshape(low, hid_shard),
            ],
            axis=1,
        )
    )
    vec_sum = jnp.concatenate([whole, part])
    nb = lax.axis_size("batch")
    vec_sum = sum_list([vec_sum] + [swap(vec_sum, "batch", m) for m in range(1, nb)])
    six = vec_sum[: 6 * shard].reshape(6, shard)
    rest = vec_sum[6 * shard :]
    return (
        decoded[None],
        tokens_grad[None],
        skip_grad[None],
        six[0],
        six[1],
        joint_grad,
        rest[:shard],
        rest[shard : 2 * shard],
        output_grad,
        six[2],
        six[3],
        six[4],
        expand_grad,
        rest[2 * shard :],
        reduce_grad,
        six[5],
        upsample_grad,
        conv_sum[:cut_one],
        conv_sum[cut_one:cut_two],
        conv_sum[cut_two:],
    )


def solution(mesh):
    rows = P("batch", "seq", None)
    vec = P("seq")
    mat = P("seq", None)
    in_specs = (rows, rows, rows, P("batch", None))
    in_specs += (vec, vec, mat, vec, vec, mat, vec, vec, vec, mat, vec, mat, vec)
    in_specs += (mat, mat, mat, mat)
    out_specs = (rows, rows, rows)
    out_specs += (vec, vec, mat, vec, vec, mat, vec, vec, vec, mat, vec, mat, vec)
    out_specs += (mat, mat, mat, mat)
    return jax.shard_map(
        on_device, mesh=mesh, in_specs=in_specs, out_specs=out_specs, check_vma=False
    )
```

time: 962 us -> 539 us (0.56)
  waiting for transfers between devices: 553 us -> 116 us
  blocking collectives: 177 us -> 0 us
  starting transfers between devices: 14.1 us -> 155 us
  local copies, waits for them, and re-layouts: 65.5 us -> 98.2 us
  other arithmetic: 29.5 us -> 60.1 us
  matrix products: 98.6 us -> 83.5 us
    reduce_scatter x8 -> x0, waiting for transfers between devices: 331 us -> none  [the longest x1 57.7 us: on_device(): lax.psum_scatter(partial_grads[9].astype(jnp.bfloat16), 'seq', scatter_di...]
    ppermute x8 -> x129, starting transfers between devices: 13.2 us -> 155 us  [the longest x121 142 us: swap(): return lax.ppermute(values, axis, [(i, i ^ mask) for i in range(count)])]
    all_gather x7 -> x2, waiting for transfers between devices: 126 us -> 0.02 us  [the longest x1 0.02 us: all_gather(): return lax.all_gather(values, 'seq', axis=0, tiled=True)]
    ppermute x8 -> x129, waiting for transfers between devices: 4.63 us -> 115 us  [the longest x121 111 us: swap(): return lax.ppermute(values, axis, [(i, i ^ mask) for i in range(count)])]
    psum x7 -> x0, blocking collectives: 97.6 us -> none  [the longest x4 53.3 us: crop_total(): return lax.psum(values, 'seq')]
    psum x1 -> x0, waiting for transfers between devices: 73.6 us -> none  [on_device(): lax.psum(group_grads[2].astype(jnp.bfloat16), 'batch').astype(jnp.float32)]
    unnamed x2 -> x0, blocking collectives: 49.1 us -> none
    all_gather x3 -> x0, blocking collectives: 30.2 us -> none  [the longest x1 11.1 us: on_device(): lax.all_gather(shards[16], 'seq', axis=0, tiled=True)]
  transfers between devices with their start and end apart: 25 -> 131, of which waited for: 18 -> 61; matrix products, arithmetic and copies ran while one was open for 11% -> 31% of each run, Pallas kernels for 0% -> 0%
where the time goes in v1:
time: 539 us; the launch traced here: 530 us
  starting transfers between devices  155 us (29%)
  waiting for transfers between devices  116 us (22%)
  local copies, waits for them, and re-layouts  98.2 us (18%)
  matrix products  83.5 us (15%)
  other arithmetic  60.1 us (11%)
  between operations  17.8 us (3%)
    ppermute x121, starting transfers between devices, swap(): return lax.ppermute(values, axis, [(i, i ^ mask) for i in range(count)])  142 us
    ppermute x121, waiting for transfers between devices, swap(): return lax.ppermute(values, axis, [(i, i ^ mask) for i in range(count)])  111 us
    dot_general x18, matrix products, bf_dot(): return jnp.dot(first_arg, second_arg, preferred_element_type=F32)  29.2 us
    unnamed x361, local copies, waits for them, and re-layouts  27.2 us
    dot_general x12, matrix products, cross_dot(): lax.dot_general(first_arg, second_arg, (((0,), (0,)), ((), ())), preferre...  18.6 us
    another operation x31, other arithmetic, gather_rel(): jnp.stack([values] + [swap(values, axis, m * stride) for m in range(1, co...  14.5 us
    slice x8, local copies, waits for them, and re-layouts, backward_taps(): turned[layer_idx].reshape(9 * weight.shape[1], in_chans)  14.2 us
  transfers between devices with their start and end apart: 131, of which 61 were waited for; matrix products, arithmetic and copies ran while one was open for 31% of the time, Pallas kernels for 0%

profile of v1, /device:TPU:0, one launch (start us, length us, event | category | flops | bytes accessed | tf_op | source)
XLA Modules:
  0.0 530.4 jit_solution(12800941611670045407)
XLA Ops:
  9.6 3.9 collective-permute-start.5
  42.9 4.7 collective-permute-start
  52.3 7.0 %collective-permute-done.1 = bf16[128,768]{1,0:T(8,128)(2,1)S(1)} collective-permute-done((bf16[128,768]{1,0:T(8,128)(2,1)S(1)}, bf16[128,768]{1,0:T(8,128)(2,1)S(1)}, u32[]{:S(2)}, u32[]{:S(2)}) %collective-permute-start.1) | collective-permute-done | bytes 196640 | tf_op jit(solution)/shard_map/ppermute | solution.py:76
  100.6 3.3 collective-permute-done.20
  104.9 3.2 collective-permute-done.21
  108.3 5.5 %multiply_convert_fusion.1 = (bf16[512,768]{1,0:T(8,128)(2,1)S(1)}, f32[512,768]{1,0:T(8,128)}, f32[512,768]{1,0:T(8,128)}) fusion(f32[768]{0:T(1024)S(1)} %copy-done.113, bf16[512,768]{1,0:T(8,128)(2,1)S(1)} %bitcast.748, bf16[768,768]{1,0:T(8,128)(2,1)S(1)} %bitcast.646), kind=kOutput, calls=%fused_computation.51 | convolution fusion | flops 629932032 | bytes 5901312 | tf_op jit(solution)/shard_map/dot_general | solution.py:25
  121.6 2.8 collective-permute-done.29
  132.0 2.7 collective-permute-done.31
  152.1 3.9 fusion.59
  156.0 3.9 convolution_add_fusion.9
  188.1 4.9 collective-permute-start.39
  248.5 2.9 collective-permute-start.49
  258.6 3.8 convolution_convert_fusion.1
  262.4 4.0 convolution_convert_fusion.2
  280.8 2.9 fusion.215
  283.6 4.0 collective-permute-start.56
  293.5 4.4 collective-permute-done.55
  309.2 3.5 collective-permute-done.57
  312.7 3.8 collective-permute-done.59
  331.5 4.0 fusion.27
  372.0 3.3 collective-permute-done.95
  381.8 4.2 collective-permute-done.105
  387.5 4.9 collective-permute-done.104
  403.1 4.0 fusion.213
  417.5 3.1 collective-permute-start.73
  427.9 2.9 collective-permute-start.107
  446.6 3.4 collective-permute-done.98
  451.4 2.7 collective-permute-done.97
  464.2 6.1 %collective-permute-done.100 = bf16[24,3072]{1,0:T(8,128)(2,1)S(1)} collective-permute-done((bf16[24,3072]{1,0:T(8,128)(2,1)S(1)}, bf16[24,3072]{1,0:T(8,128)(2,1)S(1)}, u32[]{:S(2)}, u32[]{:S(2)}) %collective-permute-start.100) | collective-permute-done | bytes 147488 | tf_op jit(solution)/shard_map/ppermute | solution.py:76
  489.8 6.1 %collective-permute-done.80 = bf16[24,2304]{1,0:T(8,128)(2,1)S(1)} collective-permute-done((bf16[24,2304]{1,0:T(8,128)(2,1)S(1)}, bf16[24,2304]{1,0:T(8,128)(2,1)S(1)}, u32[]{:S(2)}, u32[]{:S(2)}) %collective-permute-start.80) | collective-permute-done | bytes 110624 | tf_op jit(solution)/shard_map/ppermute | solution.py:76
  497.5 2.9 collective-permute-start.82
  508.1 4.8 collective-permute-done.124
  (944 shorter events, 385.2 us)
Async XLA Ops:
  7.2 118.8 %all-gather.4.cloned.1.call-start = ((), (), s32[]{:S(2)}) async-start(), calls=%async_computation | async-start | bytes 1769472 | tf_op jit(solution)/shard_map/all_gather | solution.py:250
  8.0 142.6 %all-gather.6.cloned.1.call-start = ((), (), s32[]{:S(2)}) async-start(), calls=%async_computation.1 | async-start | bytes 3059712 | tf_op jit(solution)/shard_map/all_gather | solution.py:301
  9.6 16.0 %collective-permute-start.5 = (bf16[12,96]{1,0:T(8,128)(2,1)S(1)}, bf16[12,96]{1,0:T(8,128)(2,1)S(1)}, u32[]{:S(2)}, u32[]{:S(2)}) collective-permute-start(bf16[12,96]{1,0:T(8,128)(2,1)S(1)} %concatenate.201), channel_id=1, source_target_pairs={{0,6},{1,7},{2,4},{3,5},{4,2},{5,3},{6,0},{7,1},{8,14},{9,15},{10,... | collective-permute-start | bytes 6920 | tf_op jit(solution)/shard_map/ppermute | solution.py:76
  13.5 12.2 %collective-permute-start.4 = (bf16[12,96]{1,0:T(8,128)(2,1)S(1)}, bf16[12,96]{1,0:T(8,128)(2,1)S(1)}, u32[]{:S(2)}, u32[]{:S(2)}) collective-permute-start(bf16[12,96]{1,0:T(8,128)(2,1)S(1)} %concatenate.201), channel_id=1, source_target_pairs={{0,4},{1,5},{2,6},{3,7},{4,0},{5,1},{6,2},{7,3},{8,12},{9,13},{10,... | collective-permute-start | bytes 6920 | tf_op jit(solution)/shard_map/ppermute | solution.py:76
  14.0 13.6 %collective-permute-start.3 = (bf16[12,96]{1,0:T(8,128)(2,1)S(1)}, bf16[12,96]{1,0:T(8,128)(2,1)S(1)}, u32[]{:S(2)}, u32[]{:S(2)}) collective-permute-start(bf16[12,96]{1,0:T(8,128)(2,1)S(1)} %concatenate.201), channel_id=1, source_target_pairs={{0,2},{1,3},{2,0},{3,1},{4,6},{5,7},{6,4},{7,5},{8,10},{9,11},{10,... | collective-permute-start | bytes 6920 | tf_op jit(solution)/shard_map/ppermute | solution.py:76
  14.2 24.6 %collective-permute-start.15 = (bf16[96,768]{1,0:T(8,128)(2,1)}, bf16[96,768]{1,0:T(8,128)(2,1)S(1)}, u32[]{:S(2)}, u32[]{:S(2)}) collective-permute-start(bf16[96,768]{1,0:T(8,128)(2,1)} %param.30), channel_id=1, source_target_pairs={{0,2},{1,3},{2,0},{3,1},{4,6},{5,7},{6,4},{7,5},{8,10},{9,11},{10,... | collective-permute-start | bytes 442376 | tf_op jit(solution)/shard_map/ppermute | solution.py:76
  18.7 12.4 %collective-permute-start.9 = (bf16[96,576]{0,1:T(8,128)(2,1)S(1)}, bf16[96,576]{0,1:T(8,128)(2,1)S(1)}, u32[]{:S(2)}, u32[]{:S(2)}) collective-permute-start(bf16[96,576]{0,1:T(8,128)(2,1)S(1)} %get-tuple-element.140), channel_id=1, source_target_pairs={{0,6},{1,7},{2,4},{3,5},{4,2},{5,3},{6,0},{7,1},{8,14},{9,15},{10,... | collective-permute-start | bytes 331784 | tf_op jit(solution)/shard_map/ppermute | solution.py:76
  25.8 11.5 %collective-permute-start.7 = (bf16[96,576]{0,1:T(8,128)(2,1)S(1)}, bf16[96,576]{0,1:T(8,128)(2,1)}, u32[]{:S(2)}, u32[]{:S(2)}) collective-permute-start(bf16[96,576]{0,1:T(8,128)(2,1)S(1)} %get-tuple-element.142), channel_id=1, source_target_pairs={{0,2},{1,3},{2,0},{3,1},{4,6},{5,7},{6,4},{7,5},{8,10},{9,11},{10,... | collective-permute-start | bytes 331784 | tf_op jit(solution)/shard_map/ppermute | solution.py:76
  31.0 11.8 %collective-permute-start.23 = (bf16[96,768]{1,0:T(8,128)(2,1)}, bf16[96,768]{1,0:T(8,128)(2,1)S(1)}, u32[]{:S(2)}, u32[]{:S(2)}) collective-permute-start(bf16[96,768]{1,0:T(8,128)(2,1)} %bitcast.604), channel_id=1, source_target_pairs={{0,4},{1,5},{2,6},{3,7},{4,0},{5,1},{6,2},{7,3},{8,12},{9,13},{10,... | collective-permute-start | bytes 442376 | tf_op jit(solution)/shard_map/ppermute | solution.py:76
  33.0 14.6 %collective-permute-start.24 = (bf16[96,768]{1,0:T(8,128)(2,1)}, bf16[96,768]{1,0:T(8,128)(2,1)S(1)}, u32[]{:S(2)}, u32[]{:S(2)}) collective-permute-start(bf16[96,768]{1,0:T(8,128)(2,1)} %bitcast.603), channel_id=1, source_target_pairs={{0,6},{1,7},{2,4},{3,5},{4,2},{5,3},{6,0},{7,1},{8,14},{9,15},{10,... | collective-permute-start | bytes 442376 | tf_op jit(solution)/shard_map/ppermute | solution.py:76
  37.3 13.4 %collective-permute-start.17 = (bf16[96,768]{1,0:T(8,128)(2,1)S(1)}, bf16[96,768]{1,0:T(8,128)(2,1)S(1)}, u32[]{:S(2)}, u32[]{:S(2)}) collective-permute-start(bf16[96,768]{1,0:T(8,128)(2,1)S(1)} %copy-done.78), channel_id=1, source_target_pairs={{0,6},{1,7},{2,4},{3,5},{4,2},{5,3},{6,0},{7,1},{8,14},{9,15},{10,... | collective-permute-start | bytes 442376 | tf_op jit(solution)/shard_map/ppermute | solution.py:76
  38.7 12.5 %collective-permute-start.16 = (bf16[96,768]{1,0:T(8,128)(2,1)S(1)}, bf16[96,768]{1,0:T(8,128)(2,1)S(1)}, u32[]{:S(2)}, u32[]{:S(2)}) collective-permute-start(bf16[96,768]{1,0:T(8,128)(2,1)S(1)} %copy-done.78), channel_id=1, source_target_pairs={{0,4},{1,5},{2,6},{3,7},{4,0},{5,1},{6,2},{7,3},{8,12},{9,13},{10,... | collective-permute-start | bytes 442376 | tf_op jit(solution)/shard_map/ppermute | solution.py:76
  41.0 18.4 %collective-permute-start.1 = (bf16[128,768]{1,0:T(8,128)(2,1)S(1)}, bf16[128,768]{1,0:T(8,128)(2,1)S(1)}, u32[]{:S(2)}, u32[]{:S(2)}) collective-permute-start(bf16[128,768]{1,0:T(8,128)(2,1)S(1)} %bitcast.660), channel_id=1, source_target_pairs={{0,4},{1,5},{2,6},{3,7},{4,0},{5,1},{6,2},{7,3},{8,12},{9,13},{10,... | collective-permute-start | bytes 589832 | tf_op jit(solution)/shard_map/ppermute | solution.py:76
  42.9 16.5 %collective-permute-start = (bf16[128,768]{1,0:T(8,128)(2,1)S(1)}, bf16[128,768]{1,0:T(8,128)(2,1)S(1)}, u32[]{:S(2)}, u32[]{:S(2)}) collective-permute-start(bf16[128,768]{1,0:T(8,128)(2,1)S(1)} %bitcast.661), channel_id=1, source_target_pairs={{0,2},{1,3},{2,0},{3,1},{4,6},{5,7},{6,4},{7,5},{8,10},{9,11},{10,... | collective-permute-start | bytes 589832 | tf_op jit(solution)/shard_map/ppermute | solution.py:76
  47.6 12.3 %collective-permute-start.2 = (bf16[128,768]{1,0:T(8,128)(2,1)S(1)}, bf16[128,768]{1,0:T(8,128)(2,1)S(1)}, u32[]{:S(2)}, u32[]{:S(2)}) collective-permute-start(bf16[128,768]{1,0:T(8,128)(2,1)S(1)} %bitcast.662), channel_id=1, source_target_pairs={{0,6},{1,7},{2,4},{3,5},{4,2},{5,3},{6,0},{7,1},{8,14},{9,15},{10,... | collective-permute-start | bytes 589832 | tf_op jit(solution)/shard_map/ppermute | solution.py:76
  50.7 15.6 %collective-permute-start.26 = (bf16[384,768]{1,0:T(8,128)(2,1)}, bf16[384,768]{1,0:T(8,128)(2,1)}, u32[]{:S(2)}, u32[]{:S(2)}) collective-permute-start(bf16[384,768]{1,0:T(8,128)(2,1)} %param.36), channel_id=1, source_target_pairs={{0,1},{1,0},{2,3},{3,2},{4,5},{5,4},{6,7},{7,6},{8,9},{9,8},{10,11... | collective-permute-start | bytes 1769480 | tf_op jit(solution)/shard_map/ppermute | solution.py:76
  198.1 14.5 %collective-permute-start.41 = (f32[4,8,128]{2,1,0:T(8,128)}, f32[4,8,128]{2,1,0:T(8,128)}, u32[]{:S(2)}, u32[]{:S(2)}) collective-permute-start(f32[4,8,128]{2,1,0:T(8,128)} %get-tuple-element.176), channel_id=1, source_target_pairs={{0,1},{1,0},{2,3},{3,2},{4,5},{5,4},{6,7},{7,6},{8,9},{9,8},{10,11... | collective-permute-start | bytes 49160 | tf_op jit(solution)/shard_map/ppermute | solution.py:76
  291.4 71.1 %collective-permute-start.109 = (bf16[4,96,1024]{2,1,0:T(8,128)(2,1)}, bf16[4,96,1024]{2,1,0:T(8,128)(2,1)}, u32[]{:S(2)}, u32[]{:S(2)}) collective-permute-start(bf16[4,96,1024]{2,1,0:T(8,128)(2,1)} %dynamic-slice_bitcast_fusion.1), channel_id=1, source_target_pairs={{0,1},{1,0},{2,3},{3,2},{4,5},{5,4},{6,7},{7,6},{8,9},{9,8},{10,11... | collective-permute-start | bytes 2359304 | tf_op jit(solution)/shard_map/ppermute | solution.py:76
  323.5 34.8 %collective-permute-start.102 = (bf16[384,768]{1,0:T(8,128)(2,1)}, bf16[384,768]{1,0:T(8,128)(2,1)}, u32[]{:S(2)}, u32[]{:S(2)}) collective-permute-start(bf16[384,768]{1,0:T(8,128)(2,1)} %dynamic-slice_bitcast_fusion.2), channel_id=1, source_target_pairs={{0,1},{1,0},{2,3},{3,2},{4,5},{5,4},{6,7},{7,6},{8,9},{9,8},{10,11... | collective-permute-start | bytes 1769480 | tf_op jit(solution)/shard_map/ppermute | solution.py:76
  353.9 121.8 %collective-permute-start.119 = (bf16[4,1328,128]{2,1,0:T(8,128)(2,1)}, bf16[4,1328,128]{2,1,0:T(8,128)(2,1)}, u32[]{:S(2)}, u32[]{:S(2)}) collective-permute-start(bf16[4,1328,128]{2,1,0:T(8,128)(2,1)} %dynamic-slice_bitcast_fusion), channel_id=1, source_target_pairs={{0,1},{1,0},{2,3},{3,2},{4,5},{5,4},{6,7},{7,6},{8,9},{9,8},{10,11... | collective-permute-start | bytes 4079624 | tf_op jit(solution)/shard_map/ppermute | solution.py:76
  357.5 42.9 %collective-permute-start.63 = (bf16[512,384]{1,0:T(8,128)(2,1)}, bf16[512,384]{1,0:T(8,128)(2,1)}, u32[]{:S(2)}, u32[]{:S(2)}) collective-permute-start(bf16[512,384]{1,0:T(8,128)(2,1)} %fusion.83), channel_id=1, source_target_pairs={{0,1},{1,0},{2,3},{3,2},{4,5},{5,4},{6,7},{7,6},{8,9},{9,8},{10,11... | collective-permute-start | bytes 1179656 | tf_op jit(solution)/shard_map/ppermute | solution.py:76
  379.2 13.2 %collective-permute-start.104 = (bf16[96,768]{1,0:T(8,128)(2,1)}, bf16[96,768]{1,0:T(8,128)(2,1)}, u32[]{:S(2)}, u32[]{:S(2)}) collective-permute-start(bf16[96,768]{1,0:T(8,128)(2,1)} %get-tuple-element.123), channel_id=1, source_target_pairs={{0,16},{8,24},{16,0},{24,8},{1,17},{9,25},{17,1},{25,9},{2,18},{10... | collective-permute-start | bytes 442376 | tf_op jit(solution)/shard_map/ppermute | solution.py:76
  381.2 13.7 %collective-permute-start.110 = (bf16[96,1024]{1,0:T(8,128)(2,1)}, bf16[96,1024]{1,0:T(8,128)(2,1)S(1)}, u32[]{:S(2)}, u32[]{:S(2)}) collective-permute-start(bf16[96,1024]{1,0:T(8,128)(2,1)} %get-tuple-element.77), channel_id=1, source_target_pairs={{0,2},{1,3},{2,0},{3,1},{4,6},{5,7},{6,4},{7,5},{8,10},{9,11},{10,... | collective-permute-start | bytes 589832 | tf_op jit(solution)/shard_map/ppermute | solution.py:76
  394.9 39.4 %collective-permute-start.108 = (bf16[96,768]{1,0:T(8,128)(2,1)}, bf16[96,768]{1,0:T(8,128)(2,1)}, u32[]{:S(2)}, u32[]{:S(2)}) collective-permute-start(bf16[96,768]{1,0:T(8,128)(2,1)} %fusion.106), channel_id=1, source_target_pairs={{0,24},{8,16},{16,8},{24,0},{1,25},{9,17},{17,9},{25,1},{2,26},{10... | collective-permute-start | bytes 442376 | tf_op jit(solution)/shard_map/ppermute | solution.py:76
  433.5 11.7 %collective-permute-start.96 = (bf16[24,3072]{1,0:T(8,128)(2,1)S(1)}, bf16[24,3072]{1,0:T(8,128)(2,1)S(1)}, u32[]{:S(2)}, u32[]{:S(2)}) collective-permute-start(bf16[24,3072]{1,0:T(8,128)(2,1)S(1)} %copy-done.81), channel_id=1, source_target_pairs={{0,8},{8,0},{16,24},{24,16},{1,9},{9,1},{17,25},{25,17},{2,10},{10... | collective-permute-start | bytes 442376 | tf_op jit(solution)/shard_map/ppermute | solution.py:76
  445.0 26.9 %collective-permute-start.75 = (bf16[4,96,576]{2,1,0:T(8,128)(2,1)S(1)}, bf16[4,96,576]{2,1,0:T(8,128)(2,1)S(1)}, u32[]{:S(2)}, u32[]{:S(2)}) collective-permute-start(bf16[4,96,576]{2,1,0:T(8,128)(2,1)S(1)} %dynamic-slice_bitcast_fusion.4), channel_id=1, source_target_pairs={{0,1},{1,0},{2,3},{3,2},{4,5},{5,4},{6,7},{7,6},{8,9},{9,8},{10,11... | collective-permute-start | bytes 1327112 | tf_op jit(solution)/shard_map/ppermute | solution.py:76
  445.2 12.1 %collective-permute-start.64 = (bf16[128,768]{1,0:T(8,128)(2,1)S(1)}, bf16[128,768]{1,0:T(8,128)(2,1)S(1)}, u32[]{:S(2)}, u32[]{:S(2)}) collective-permute-start(bf16[128,768]{1,0:T(8,128)(2,1)S(1)} %get-tuple-element.80), channel_id=1, source_target_pairs={{0,2},{1,3},{2,0},{3,1},{4,6},{5,7},{6,4},{7,5},{8,10},{9,11},{10,... | collective-permute-start | bytes 589832 | tf_op jit(solution)/shard_map/ppermute | solution.py:76
  459.2 11.2 %collective-permute-start.100 = (bf16[24,3072]{1,0:T(8,128)(2,1)S(1)}, bf16[24,3072]{1,0:T(8,128)(2,1)S(1)}, u32[]{:S(2)}, u32[]{:S(2)}) collective-permute-start(bf16[24,3072]{1,0:T(8,128)(2,1)S(1)} %fusion.109), channel_id=1, source_target_pairs={{0,16},{8,24},{16,0},{24,8},{1,17},{9,25},{17,1},{25,9},{2,18},{10... | collective-permute-start | bytes 442376 | tf_op jit(solution)/shard_map/ppermute | solution.py:76
  483.3 12.6 %collective-permute-start.80 = (bf16[24,2304]{1,0:T(8,128)(2,1)S(1)}, bf16[24,2304]{1,0:T(8,128)(2,1)S(1)}, u32[]{:S(2)}, u32[]{:S(2)}) collective-permute-start(bf16[24,2304]{1,0:T(8,128)(2,1)S(1)} %get-tuple-element.153), channel_id=1, source_target_pairs={{0,16},{8,24},{16,0},{24,8},{1,17},{9,25},{17,1},{25,9},{2,18},{10... | collective-permute-start | bytes 331784 | tf_op jit(solution)/shard_map/ppermute | solution.py:76
  485.0 12.5 %collective-permute-start.120 = (bf16[1328,128]{1,0:T(8,128)(2,1)S(1)}, bf16[1328,128]{1,0:T(8,128)(2,1)S(1)}, u32[]{:S(2)}, u32[]{:S(2)}) collective-permute-start(bf16[1328,128]{1,0:T(8,128)(2,1)S(1)} %get-tuple-element.68), channel_id=1, source_target_pairs={{0,2},{1,3},{2,0},{3,1},{4,6},{5,7},{6,4},{7,5},{8,10},{9,11},{10,... | collective-permute-start | bytes 1019912 | tf_op jit(solution)/shard_map/ppermute | solution.py:76
  486.3 14.1 %collective-permute-start.122 = (bf16[1328,128]{1,0:T(8,128)(2,1)S(1)}, bf16[1328,128]{1,0:T(8,128)(2,1)S(1)}, u32[]{:S(2)}, u32[]{:S(2)}) collective-permute-start(bf16[1328,128]{1,0:T(8,128)(2,1)S(1)} %get-tuple-element.69), channel_id=1, source_target_pairs={{0,6},{1,7},{2,4},{3,5},{4,2},{5,3},{6,0},{7,1},{8,14},{9,15},{10,... | collective-permute-start | bytes 1019912 | tf_op jit(solution)/shard_map/ppermute | solution.py:76
  488.5 11.9 %collective-permute-start.121 = (bf16[1328,128]{1,0:T(8,128)(2,1)S(1)}, bf16[1328,128]{1,0:T(8,128)(2,1)S(1)}, u32[]{:S(2)}, u32[]{:S(2)}) collective-permute-start(bf16[1328,128]{1,0:T(8,128)(2,1)S(1)} %get-tuple-element.70), channel_id=1, source_target_pairs={{0,4},{1,5},{2,6},{3,7},{4,0},{5,1},{6,2},{7,3},{8,12},{9,13},{10,... | collective-permute-start | bytes 1019912 | tf_op jit(solution)/shard_map/ppermute | solution.py:76
  (226 other events, 1848.3 us)
Sparse Core Ops, SparseCore 0:
  9.9 34.4 all-gather.3
  46.9 35.9 all-gather.5
